TPU v7x, 1024 devices: a whole 8x8x8 slice. The times are simulated.
1024 devices in a mesh: row: 128 (over y, x, core), col: 8 (over z).
Axes of the slice: x: 8, y: 8, z: 8, core: 2. Of those that a mesh axis runs over, the one named last changes fastest.
Arguments:
- features: bfloat16 [8, 128, 16, 512], P('col', 'row'), may hold values from -6 to 6
- weight: bfloat16 [512, 512], replicated, may hold values from -0.25 to 0.25
- cotangent: bfloat16 [128, 8, 16, 512], P('row', 'col'), may hold values from -6 to 6
- tile_mask: int32 [128, 8, 12, 128, 128], P('row', 'col'), may hold values 0 or 1
- tile_cols: int32 [128, 8, 12], P('row', 'col'), may hold values from 0 to 15, as said below
- tile_count: int32 [128, 8], P('row', 'col'), may hold values from 3 to 12, as said below
- degree: int32 [128, 128], P('row'), may hold values from 384 to 3073
Outputs:
- activated: bfloat16 [128, 8, 16, 512], P('row', 'col')
- feature_grad: bfloat16 [8, 128, 16, 512], P('col', 'row')
- weight_grad: float32 [512, 512], P('col')
Inputs may be any that keep to these rules, and one draw needn't show every extreme that they name: `tile_cols`: within one block the 12 tile columns are distinct. Only the first tile_count[r, c] slots of a block are live; in every draw some whole row of blocks has all 12 slots live.
All inputs are finite; a program needn't handle non-finite values. No bound on the sum of `tile_mask` on one device may be relied on, other than what follows from the above.
Results may differ from a plain program's by a relative error of at most 0.007.
Values may be sent and summed in bfloat16 or wider, within the bound.
No kernel may reach another device: no remote copies, remote signals or barrier semaphores. Data moves between devices by JAX's collectives and lax.ppermute only.
A program may use at most 32 MiB of HBM per device.

v0:
```python
import jax
import jax.numpy as jnp
from jax import lax
from jax.sharding import PartitionSpec as P


def slope_of(preact):
    sigma = jax.nn.sigmoid(preact)
    return sigma * (1.0 + preact * (1.0 - sigma))


def reduce_weight(weight_term):
    col_share = lax.psum_scatter(weight_term, "col", scatter_dimension=0, tiled=True)
    return lax.psum(col_share, "row")


def body(features, weight, cotangent, tile_mask, tile_cols, tile_count, degree):
    node_rows = features.shape[2]
    width = features.shape[3]
    tile_slots = tile_cols.shape[2]
    block_rows = tile_mask.shape[3]
    tile_width = tile_mask.shape[4]
    panel_count = node_rows * lax.axis_size("row") // tile_width
    live_count = tile_count[0, 0]
    slot_cols = tile_cols[0, 0]
    live_tiles = (jnp.arange(tile_slots, dtype=jnp.int32) < live_count).astype(jnp.float32)
    onehot = (slot_cols[:, None] == jnp.arange(panel_count, dtype=jnp.int32)[None, :]).astype(
        jnp.float32
    )
    onehot = onehot * live_tiles[:, None]
    masks = tile_mask[0, 0].astype(jnp.float32)
    row_scale = lax.rsqrt(degree[0].astype(jnp.float32))
    counts = jnp.einsum("kp,kit->ipt", onehot, masks).reshape(block_rows, panel_count * tile_width)
    dense_block = (counts * row_scale[:, None]).astype(jnp.bfloat16)
    piece_rows = lax.all_gather(features, "row", axis=1, tiled=True).reshape(-1, width)
    block_cols = dense_block
    partial_sum = jnp.dot(block_cols, piece_rows, preferred_element_type=jnp.float32)
    contract_rows = (((0,), (0,)), ((), ()))
    own_sum = lax.psum_scatter(partial_sum, "col", scatter_dimension=0, tiled=True)
    own_inputs = own_sum.astype(jnp.bfloat16)
    own_pre = jnp.dot(own_inputs, weight, preferred_element_type=jnp.float32)
    activated = jax.nn.silu(own_pre).astype(jnp.bfloat16)
    own_slope = (cotangent[0, 0].astype(jnp.float32) * slope_of(own_pre)).astype(jnp.bfloat16)
    block_slope = lax.all_gather(own_slope, "col", axis=0, tiled=True)
    weight_term = lax.dot_general(
        own_inputs, own_slope, contract_rows, preferred_element_type=jnp.float32
    )
    weight_grad = reduce_weight(weight_term)
    projected = jnp.dot(block_slope, weight.T, preferred_element_type=jnp.float32).astype(
        jnp.bfloat16
    )
    block_cols = dense_block
    grad_rows = lax.psum_scatter(
        lax.dot_general(block_cols, projected, contract_rows, preferred_element_type=jnp.float32),
        "row",
        scatter_dimension=0,
        tiled=True,
    )
    feature_grad = grad_rows.astype(jnp.bfloat16).reshape(1, 1, node_rows, width)
    return (activated.reshape(1, 1, node_rows, width), feature_grad, weight_grad)


def solution(mesh):
    in_specs = (
        P("col", "row", None, None),
        P(),
        P("row", "col", None, None),
        P("row", "col", None, None, None),
        P("row", "col", None),
        P("row", "col"),
        P("row", None),
    )
    out_specs = (P("row", "col", None, None), P("col", "row", None, None), P("col", None))
    return jax.shard_map(body, mesh=mesh, in_specs=in_specs, out_specs=out_specs, check_vma=False)
```

profile of v0, /device:TPU:1, one launch (start us, length us, event | category | flops | bytes accessed | tf_op | source)
XLA Modules:
  0.0 622.9 jit_solution(14937235555184811577)
XLA Ops:
  7.2 0.0 copy-start
  7.2 0.0 all-gather.2.cloned.1.call-start
  7.2 0.7 all-gather.2.cloned.1.call-update
  7.9 0.0 reduce-scatter.4.cloned.1.call-start
  8.6 0.7 rsqrt_bitcast_fusion
  9.3 1.2 convert_bitcast_fusion
  10.5 1.0 fusion.2
  11.5 0.0 copy-start.1
  11.5 100.9 %all-gather.2.cloned.1.call-done = bf16[1,128,16,512]{3,2,0,1:T(8,128)(2,1)} async-done(((bf16[1,1,16,512]{3,2,0,1:T(8,128)(2,1)}), bf16[1,128,16,512]{3,2,0,1:T(8,128)(2,1)}) %all-gather.2.cloned.1.call-update) | async-done | bytes 2097168 | tf_op jit(solution)/shard_map/all_gather | solution.py:35
  112.4 2.7 fusion.6
  115.2 0.0 reduce-scatter.4.cloned.1.call-update
  115.2 0.0 reduce-scatter.8.cloned.1.call-start
  115.3 37.2 %reduce-scatter.4.cloned.1.call-done = f32[16,512]{1,0:T(8,128)} async-done(((f32[128,512]{1,0:T(8,128)}), f32[16,512]{1,0:T(8,128)}) %reduce-scatter.4.cloned.1.call-update) | async-done | bytes 32784 | tf_op jit(solution)/shard_map/reduce_scatter | solution.py:39
  152.5 0.0 copy-done
  152.5 0.0 copy-done.1
  152.5 1.6 fusion.10
  154.0 2.0 fusion.13
  156.1 0.0 reduce-scatter.8.cloned.1.call-update
  156.1 0.0 reduce-scatter.6.cloned.1.call-start
  156.2 18.5 %all_gather.7 = bf16[128,512]{1,0:T(8,128)(2,1)S(1)} all-gather(bf16[16,512]{1,0:T(8,128)(2,1)S(1)} %get-tuple-element.3), channel_id=1, replica_groups=mesh['row'=128,'col'=8] {'col'}, dimensions={0}, use_global_device_ids=true | all-gather | bytes 147456 | tf_op jit(solution)/shard_map/all_gather | solution.py:44
  174.7 3.0 fusion
  177.7 0.0 reduce-scatter.6.cloned.1.call-update
  177.7 0.0 all-reduce.2.cloned.1.call-start
  177.8 23.2 %reduce-scatter.8.cloned.1.call-done = f32[64,512]{1,0:T(8,128)} async-done(((f32[512,512]{1,0:T(8,128)}), f32[64,512]{1,0:T(8,128)}) %reduce-scatter.8.cloned.1.call-update) | async-done | bytes 131088 | tf_op jit(solution)/shard_map/reduce_scatter | solution.py:13
  200.9 0.0 all-reduce.2.cloned.1.call-update
  201.0 213.2 %reduce-scatter.6.cloned.1.call-done = f32[16,512]{1,0:T(8,128)} async-done(((f32[2048,512]{1,0:T(8,128)}), f32[16,512]{1,0:T(8,128)}) %reduce-scatter.6.cloned.1.call-update) | async-done | bytes 32784 | tf_op jit(solution)/shard_map/reduce_scatter | solution.py:53
  414.2 1.4 convert_bitcast_fusion.1
  415.6 199.3 %all-reduce.2.cloned.1.call-done = f32[64,512]{1,0:T(8,128)} async-done(((f32[64,512]{1,0:T(8,128)}), f32[64,512]{1,0:T(8,128)}) %all-reduce.2.cloned.1.call-update) | async-done | bytes 131088 | tf_op jit(solution)/shard_map/psum | solution.py:14
  614.8 1.6 copy.27
  (1 shorter events, 0.0 us)
Async XLA Ops:
  7.2 145.3 %copy-start = (bf16[512,512]{1,0:T(8,128)(2,1)S(1)}, bf16[512,512]{1,0:T(8,128)(2,1)}, u32[]{:S(2)}) copy-start(bf16[512,512]{1,0:T(8,128)(2,1)} %param.8) | copy-start | bytes 1572868
  7.2 105.3 %all-gather.2.cloned.1.call-start = ((), (), s32[]{:S(2)}) async-start(), calls=%async_computation.3 | async-start | bytes 2113536 | tf_op jit(solution)/shard_map/all_gather | solution.py:35
  7.9 144.6 %reduce-scatter.4.cloned.1.call-start = ((), (), s32[]{:S(2)}) async-start(), calls=%async_computation.4 | async-start | bytes 294912 | tf_op jit(solution)/shard_map/reduce_scatter | solution.py:39
  11.5 140.9 %copy-start.1 = (bf16[1,1,16,512]{3,2,1,0:T(8,128)(2,1)S(1)}, bf16[1,1,16,512]{3,2,1,0:T(8,128)(2,1)}, u32[]{:S(2)}) copy-start(bf16[1,1,16,512]{3,2,1,0:T(8,128)(2,1)} %param.9) | copy-start | bytes 49156
  115.2 85.7 %reduce-scatter.8.cloned.1.call-start = ((), (), s32[]{:S(2)}) async-start(), calls=%async_computation.6 | async-start | bytes 1179648 | tf_op jit(solution)/shard_map/reduce_scatter | solution.py:13
  156.1 258.1 %reduce-scatter.6.cloned.1.call-start = ((), (), s32[]{:S(2)}) async-start(), calls=%async_computation.5 | async-start | bytes 4227072 | tf_op jit(solution)/shard_map/reduce_scatter | solution.py:53
  177.7 437.1 %all-reduce.2.cloned.1.call-start = ((), (), s32[]{:S(2)}) async-start(), calls=%async_computation.7 | async-start | bytes 262144 | tf_op jit(solution)/shard_map/psum | solution.py:14
Sparse Core Ops, SparseCore 0:
  12.3 100.0 all-gather.1
  115.8 36.6 reduce-scatter.3
  156.3 44.6 reduce-scatter.7
  207.3 206.8 reduce-scatter.5
  417.3 197.4 all-reduce.1
where the time goes:
time: 623 us
  waiting for transfers between devices  575 us (92%)
  blocking collectives  18.5 us (3%)
  between operations  14.5 us (2%)
  matrix products  10.4 us (2%)
    reduce_scatter x1, waiting for transfers between devices, body(): lax.psum_scatter(lax.dot_general(block_cols, projected, contract_rows, pr...  213 us
    psum x1, waiting for transfers between devices, reduce_weight(): return lax.psum(col_share, 'row')  199 us
    all_gather x1, waiting for transfers between devices, body(): lax.all_gather(features, 'row', axis=1, tiled=True).reshape(-1, width)  101 us
    reduce_scatter x1, waiting for transfers between devices, body(): lax.psum_scatter(partial_sum, 'col', scatter_dimension=0, tiled=True)  37.2 us
    reduce_scatter x1, waiting for transfers between devices, reduce_weight(): lax.psum_scatter(weight_term, 'col', scatter_dimension=0, tiled=True)  23.2 us
    all_gather x1, blocking collectives, body(): block_slope = lax.all_gather(own_slope, 'col', axis=0, tiled=True)  18.5 us
  transfers between devices with their start and end apart: 5, of which 5 were waited for; matrix products, arithmetic and copies ran while one was open for 1% of the time, Pallas kernels for 0%

commit v1 on v0

v1 whole, which is shorter than its diff:
```python
import jax
import jax.numpy as jnp
from jax import lax
from jax.sharding import Mesh, PartitionSpec as P

ROW = ("y", "xh", "xl", "core")
CHIPS = ("y", "xh", "xl")
GROUP = ("xl", "core")
TEAM = ("xl", "core", "z")
SWAP = [(0, 1), (1, 0)]
MEMBERS = 4


def slope_of(preact):
    sigma = jax.nn.sigmoid(preact)
    return sigma * (1.0 + preact * (1.0 - sigma))


def exclusive(blocks):
    core = lax.axis_index("core") == 1
    half = lax.axis_index("xl") == 1
    a, b, c, d = (blocks[i] for i in range(MEMBERS))
    a, b, c, d = (
        jnp.where(core, b, a),
        jnp.where(core, a, b),
        jnp.where(core, d, c),
        jnp.where(core, c, d),
    )
    return [
        jnp.where(half, c, a),
        jnp.where(half, d, b),
        jnp.where(half, a, c),
        jnp.where(half, b, d),
    ]


def dense_of(tile_mask, tile_cols, tile_count, degree, panel_count):
    slots, block_rows, tile_width = tile_mask.shape
    live = (jnp.arange(slots, dtype=jnp.int32) < tile_count).astype(jnp.float32)
    onehot = (tile_cols[:, None] == jnp.arange(panel_count, dtype=jnp.int32)[None, :]).astype(
        jnp.float32
    )
    onehot = onehot * live[:, None]
    counts = jnp.einsum("kp,kit->ipt", onehot, tile_mask.astype(jnp.float32))
    counts = counts.reshape(block_rows, panel_count * tile_width)
    return (counts * lax.rsqrt(degree.astype(jnp.float32))[:, None]).astype(jnp.bfloat16)


def body(features, weight, cotangent, tile_mask, tile_cols, tile_count, degree):
    f32, bf16 = jnp.float32, jnp.bfloat16
    node_rows, width = features.shape[2], features.shape[3]
    rows = lax.axis_size(ROW)
    depth = lax.axis_size("z")
    chips = lax.axis_size(CHIPS)
    part = width // MEMBERS
    col_nodes = rows * node_rows
    block_rows = tile_mask.shape[3]

    own = features[0, 0].reshape(node_rows, MEMBERS, part).transpose(1, 0, 2)
    send = jnp.broadcast_to(own[None], (rows // MEMBERS, MEMBERS, node_rows, part))
    panels = lax.all_to_all(send.reshape(rows, node_rows, part), ROW, 0, 0)
    panels = panels.reshape(col_nodes, part)

    dense = dense_of(
        tile_mask[0, 0], tile_cols[0, 0], tile_count[0, 0], degree[0], col_nodes // tile_mask.shape[4]
    )
    across = lax.ppermute(dense, "xl", SWAP)
    blocks = [dense, lax.ppermute(dense, "core", SWAP), across, lax.ppermute(across, "core", SWAP)]

    partial = [jnp.dot(b, panels, preferred_element_type=f32).astype(bf16) for b in blocks]
    partial = jnp.stack(exclusive(partial)).reshape(MEMBERS * depth, node_rows, part)
    sums = lax.all_to_all(partial, TEAM, 0, 0).reshape(MEMBERS, depth, node_rows, part)
    sums = jnp.sum(sums.astype(f32), axis=1)
    own_inputs = jnp.concatenate([sums[m] for m in range(MEMBERS)], axis=1).astype(bf16)

    own_pre = jnp.dot(own_inputs, weight, preferred_element_type=f32)
    activated = jax.nn.silu(own_pre).astype(bf16)
    own_slope = (cotangent[0, 0].astype(f32) * slope_of(own_pre)).astype(bf16)
    own_proj = lax.dot_general(
        own_slope, weight, (((1,), (1,)), ((), ())), preferred_element_type=f32
    ).astype(bf16)

    lanes = 128
    share = width // depth
    per_lane = lanes // share
    quarters = jnp.stack(
        [
            jnp.concatenate(
                [own_proj[:, m * part : (m + 1) * part], own_slope[:, m * part : (m + 1) * part]], axis=1
            )
            for m in range(MEMBERS)
        ]
    )
    slices = jnp.stack(
        [own_inputs[:, (d // per_lane) * lanes : (d // per_lane + 1) * lanes] for d in range(depth)]
    )
    both = jnp.concatenate(
        [
            jnp.broadcast_to(quarters[:, None], (MEMBERS, depth, node_rows, 2 * part)),
            jnp.broadcast_to(slices[None], (MEMBERS, depth, node_rows, lanes)),
        ],
        axis=3,
    ).reshape(MEMBERS * depth, node_rows, 2 * part + lanes)
    both = lax.all_to_all(both, TEAM, 0, 0).reshape(MEMBERS * block_rows, 2 * part + lanes)
    proj = exclusive(both[:, :part].reshape(MEMBERS, block_rows, part))
    contract_rows = (((0,), (0,)), ((), ()))
    grad = sum(
        lax.dot_general(b, p, contract_rows, preferred_element_type=f32)
        for b, p in zip(blocks, proj, strict=True)
    )
    grad = grad.astype(bf16).reshape(rows, node_rows, part)
    term = lax.dot_general(
        both[:, 2 * part :], both[:, part : 2 * part], contract_rows, preferred_element_type=f32
    )
    term = term.reshape(per_lane, share, part)
    term = lax.dynamic_index_in_dim(term, lax.axis_index("z") % per_lane, 0, keepdims=False)
    extra = 8
    term = jnp.broadcast_to(
        term.astype(bf16)[:, None, None, :], (chips, rows // chips, extra, part)
    ).reshape(rows, extra, part)
    out = lax.all_to_all(jnp.concatenate([grad, term], axis=1), ROW, 0, 0)
    out = out.reshape(rows // MEMBERS, MEMBERS, node_rows + extra, part)
    total = jnp.sum(out[:, :, :node_rows].astype(f32), axis=0)
    feature_grad = jnp.concatenate([total[m] for m in range(MEMBERS)], axis=1).astype(bf16)
    weight_row = jnp.sum(out[:, :, node_rows].astype(f32), axis=0).reshape(1, 1, width)
    weight_grad = lax.all_to_all(jnp.broadcast_to(weight_row, (chips, 1, width)), CHIPS, 0, 0)
    return (
        activated.reshape(1, 1, node_rows, width),
        feature_grad.reshape(1, 1, node_rows, width),
        weight_grad.reshape(chips, width),
    )


def solution(mesh):
    fine = Mesh(mesh.devices.reshape(8, 4, 2, 2, 8), ("y", "xh", "xl", "core", "z"))
    in_specs = (
        P("z", ROW, None, None),
        P(),
        P(ROW, "z", None, None),
        P(ROW, "z", None, None, None),
        P(ROW, "z", None),
        P(ROW, "z"),
        P(ROW, None),
    )
    out_specs = (P(ROW, "z", None, None), P("z", ROW, None, None), P("z", None))
    return jax.shard_map(body, mesh=fine, in_specs=in_specs, out_specs=out_specs, check_vma=False)
```

time: 623 us -> 153 us (0.25)
  waiting for transfers between devices: 575 us -> 39.6 us
  blocking collectives: 18.5 us -> 62.1 us
  starting transfers between devices: 0.2 us -> 37.3 us
  between operations: 14.5 us -> 1.66 us
    reduce_scatter x3 -> x0, waiting for transfers between devices: 274 us -> none  [the longest x1 213 us: body(): lax.psum_scatter(lax.dot_general(block_cols, projected, contract_rows, pr...]
    psum x1 -> x0, waiting for transfers between devices: 199 us -> none  [reduce_weight(): return lax.psum(col_share, 'row')]
    all_gather x1 -> x0, waiting for transfers between devices: 101 us -> none  [body(): lax.all_gather(features, 'row', axis=1, tiled=True).reshape(-1, width)]
    all_to_all x0 -> x2, blocking collectives: none -> 62.1 us  [the longest x1 40.8 us: body(): out = lax.all_to_all(jnp.concatenate([grad, term], axis=1), ROW, 0, 0)]
    all_to_all x0 -> x3, starting transfers between devices: none -> 28.7 us  [the longest x1 19.4 us: body(): panels = lax.all_to_all(send.reshape(rows, node_rows, part), ROW, 0, 0)]
    all_to_all x0 -> x3, waiting for transfers between devices: none -> 23.9 us  [the longest x1 12.9 us: body(): lax.all_to_all(both, TEAM, 0, 0)]
    all_gather x1 -> x0, blocking collectives: 18.5 us -> none  [body(): block_slope = lax.all_gather(own_slope, 'col', axis=0, tiled=True)]
    ppermute x0 -> x3, waiting for transfers between devices: none -> 15.7 us  [the longest x1 15.7 us: body(): across = lax.ppermute(dense, 'xl', SWAP)]
  transfers between devices with their start and end apart: 5 -> 6, of which waited for: 5 -> 3; matrix products, arithmetic and copies ran while one was open for 1% -> 3% of each run, Pallas kernels for 0% -> 0%
where the time goes in v1:
time: 153 us; the launch traced here: 152 us
  blocking collectives  62.1 us (41%)
  waiting for transfers between devices  39.6 us (26%)
  starting transfers between devices  37.3 us (24%)
  matrix products  5.99 us (4%)
  local copies, waits for them, and re-layouts  3.35 us (2%)
  other arithmetic  2.24 us (1%)
  between operations  1.66 us (1%)
    all_to_all x1, blocking collectives, body(): out = lax.all_to_all(jnp.concatenate([grad, term], axis=1), ROW, 0, 0)  40.8 us
    all_to_all x1, blocking collectives, body(): lax.all_to_all(partial, TEAM, 0, 0).reshape(MEMBERS, depth, node_rows, part)  21.3 us
    all_to_all x1, starting transfers between devices, body(): panels = lax.all_to_all(send.reshape(rows, node_rows, part), ROW, 0, 0)  19.4 us
    ppermute x1, waiting for transfers between devices, body(): across = lax.ppermute(dense, 'xl', SWAP)  15.7 us
    all_to_all x1, waiting for transfers between devices, body(): lax.all_to_all(both, TEAM, 0, 0)  12.9 us
    all_to_all x1, waiting for transfers between devices, body(): lax.all_to_all(jnp.broadcast_to(weight_row, (chips, 1, width)), CHIPS, 0, 0)  10.9 us
    all_to_all x1, starting transfers between devices, body(): lax.all_to_all(both, TEAM, 0, 0)  4.66 us
    all_to_all x1, starting transfers between devices, body(): lax.all_to_all(jnp.broadcast_to(weight_row, (chips, 1, width)), CHIPS, 0, 0)  4.62 us
  transfers between devices with their start and end apart: 6, of which 3 were waited for; matrix products, arithmetic and copies ran while one was open for 3% of the time, Pallas kernels for 0%

profile of v1, /device:TPU:1, one launch (start us, length us, event | category | flops | bytes accessed | tf_op | source)
XLA Modules:
  0.0 152.3 jit_solution(4185970338866417466)
XLA Ops:
  0.7 0.8 reshape_squeeze.3
  1.5 0.9 broadcast_in_dim.16
  2.4 19.4 %all-to-all-start = ((bf16[128,16,128]{2,1,0:T(8,128)(2,1)}), bf16[128,16,128]{2,1,0:T(8,128)(2,1)S(1)}, u32[]{:S(2)}, u32[]{:S(2)}) async-start(bf16[128,16,128]{2,1,0:T(8,128)(2,1)} %bitcast.7), calls=%async_computation | async-start | bytes 1048576 | tf_op jit(solution)/shard_map/all_to_all | solution.py:61
  22.7 1.2 fusion.2
  23.8 0.4 fusion.1
  24.3 3.3 %collective-permute-start = (bf16[128,2048]{1,0:T(8,128)(2,1)S(1)}, bf16[128,2048]{1,0:T(8,128)(2,1)S(1)}, u32[]{:S(2)}, u32[]{:S(2)}) collective-permute-start(bf16[128,2048]{1,0:T(8,128)(2,1)S(1)} %fusion.1), channel_id=1, source_target_pairs={{0,16},{16,0},{1,17},{17,1},{2,18},{18,2},{3,19},{19,3},{4,20},{20... | collective-permute-start | bytes 1572872 | tf_op jit(solution)/shard_map/ppermute | solution.py:67
  27.6 2.5 %collective-permute-start.2 = (bf16[128,2048]{1,0:T(8,128)(2,1)S(1)}, bf16[128,2048]{1,0:T(8,128)(2,1)S(1)}, u32[]{:S(2)}, u32[]{:S(2)}) collective-permute-start(bf16[128,2048]{1,0:T(8,128)(2,1)S(1)} %fusion.1), channel_id=1, source_target_pairs={{0,8},{8,0},{1,9},{9,1},{2,10},{10,2},{3,11},{11,3},{4,12},{12,4},... | collective-permute-start | bytes 1572872 | tf_op jit(solution)/shard_map/ppermute | solution.py:68
  30.1 15.7 %collective-permute-done = bf16[128,2048]{1,0:T(8,128)(2,1)S(1)} collective-permute-done((bf16[128,2048]{1,0:T(8,128)(2,1)S(1)}, bf16[128,2048]{1,0:T(8,128)(2,1)S(1)}, u32[]{:S(2)}, u32[]{:S(2)}) %collective-permute-start) | collective-permute-done | bytes 524320 | tf_op jit(solution)/shard_map/ppermute | solution.py:67
  45.8 2.8 %collective-permute-start.1 = (bf16[128,2048]{1,0:T(8,128)(2,1)S(1)}, bf16[128,2048]{1,0:T(8,128)(2,1)S(1)}, u32[]{:S(2)}, u32[]{:S(2)}) collective-permute-start(bf16[128,2048]{1,0:T(8,128)(2,1)S(1)} %collective-permute-done), channel_id=1, source_target_pairs={{0,8},{8,0},{1,9},{9,1},{2,10},{10,2},{3,11},{11,3},{4,12},{12,4},... | collective-permute-start | bytes 1572872 | tf_op jit(solution)/shard_map/ppermute | solution.py:68
  48.6 1.3 convolution_convert_fusion
  50.0 0.3 convolution_convert_fusion.2
  50.3 0.3 convolution_convert_fusion.1
  50.6 0.3 select_bitcast_fusion.3
  50.9 21.3 %all_to_all.25 = bf16[32,16,128]{2,1,0:T(8,128)(2,1)S(1)} all-to-all(bf16[32,16,128]{2,1,0:T(8,128)(2,1)S(1)} %bitcast.109), channel_id=1, replica_groups=mesh['y'=8,'xh'=4,'xl'=2,'core'=2,'z'=8] {'xl','core','z'}, dimensions={0} | all-to-all | bytes 262144 | tf_op jit(solution)/shard_map/all_to_all | solution.py:72
  72.4 0.8 fusion.11
  73.2 0.2 convolution_convert_fusion.4
  73.5 0.8 pad_maximum_fusion.1
  74.3 4.7 %all-to-all-start.2 = ((bf16[32,16,384]{2,1,0:T(8,128)(2,1)}), bf16[32,16,384]{2,1,0:T(8,128)(2,1)S(1)}, u32[]{:S(2)}, u32[]{:S(2)}) async-start(bf16[32,16,384]{2,1,0:T(8,128)(2,1)} %bitcast.25), calls=%async_computation.2 | async-start | bytes 786432 | tf_op jit(solution)/shard_map/all_to_all | solution.py:104
  79.0 12.9 %all-to-all-done.2 = bf16[32,16,384]{2,1,0:T(8,128)(2,1)S(1)} async-done(((bf16[32,16,384]{2,1,0:T(8,128)(2,1)}), bf16[32,16,384]{2,1,0:T(8,128)(2,1)S(1)}, u32[]{:S(2)}, u32[]{:S(2)}) %all-to-all-start.2) | async-done | bytes 393248 | tf_op jit(solution)/shard_map/all_to_all | solution.py:104
  91.9 0.3 fusion.15
  92.3 0.2 fusion.7
  92.5 0.3 convolution_add_fusion.2
  92.9 0.3 convolution_add_fusion.1
  93.2 0.3 fusion
  93.6 0.1 pad_maximum_fusion
  93.8 40.8 %all_to_all.26 = bf16[128,24,128]{2,1,0:T(8,128)(2,1)S(1)} all-to-all(bf16[128,24,128]{2,1,0:T(8,128)(2,1)S(1)} %pad_maximum_fusion), channel_id=1, replica_groups=mesh['y'=8,'xh'=4,'xl'=2,'core'=2,'z'=8] {'y','xh','xl','core'}, dimensions={0} | all-to-all | bytes 1572864 | tf_op jit(solution)/shard_map/all_to_all | solution.py:121
  134.7 0.1 slice_reduce_fusion
  134.7 0.7 broadcast_in_dim.45
  135.5 4.6 %all-to-all-start.4 = ((f32[64,1,512]{2,1,0:T(1,128)}), f32[64,1,512]{2,1,0:T(1,128)S(1)}, u32[]{:S(2)}, u32[]{:S(2)}) async-start(f32[64,1,512]{2,1,0:T(1,128)} %broadcast_in_dim.45), calls=%async_computation.4 | async-start | bytes 262144 | tf_op jit(solution)/shard_map/all_to_all | solution.py:126
  140.1 0.6 pad_maximum_fusion.4
  140.7 10.9 %all-to-all-done.4 = f32[64,1,512]{2,1,0:T(1,128)S(1)} async-done(((f32[64,1,512]{2,1,0:T(1,128)}), f32[64,1,512]{2,1,0:T(1,128)S(1)}, u32[]{:S(2)}, u32[]{:S(2)}) %all-to-all-start.4) | async-done | bytes 131104 | tf_op jit(solution)/shard_map/all_to_all | solution.py:126
  151.6 0.7 copy.27
  (36 shorter events, 0.4 us)
Async XLA Ops:
  0.6 71.7 %copy-start = (bf16[512,512]{1,0:T(8,128)(2,1)S(1)}, bf16[512,512]{1,0:T(8,128)(2,1)}, u32[]{:S(2)}) copy-start(bf16[512,512]{1,0:T(8,128)(2,1)} %param.8) | copy-start | bytes 1572868
  0.6 21.2 %copy-start.4 = (s32[1,128]{1,0:T(1,128)S(1)}, s32[1,128]{1,0:T(1,128)}, u32[]{:S(2)}) copy-start(s32[1,128]{1,0:T(1,128)} %param.13) | copy-start | bytes 1540
  0.7 21.3 %copy-start.1 = (s32[1,1,12,128,128]{4,3,2,1,0:T(8,128)S(1)}, s32[1,1,12,128,128]{4,3,2,1,0:T(8,128)}, u32[]{:S(2)}) copy-start(s32[1,1,12,128,128]{4,3,2,1,0:T(8,128)} %param.10) | copy-start | bytes 2359300
  2.4 20.2 %copy-start.3 = (s32[1,1,12]{2,1,0:T(1,128)S(1)}, s32[1,1,12]{2,1,0:T(1,128)}, u32[]{:S(2)}) copy-start(s32[1,1,12]{2,1,0:T(1,128)} %param.11) | copy-start | bytes 148
  2.4 46.2 %all-to-all-start = ((bf16[128,16,128]{2,1,0:T(8,128)(2,1)}), bf16[128,16,128]{2,1,0:T(8,128)(2,1)S(1)}, u32[]{:S(2)}, u32[]{:S(2)}) async-start(bf16[128,16,128]{2,1,0:T(8,128)(2,1)} %bitcast.7), calls=%async_computation | async-start | bytes 1048576 | tf_op jit(solution)/shard_map/all_to_all | solution.py:61
  24.3 21.6 %collective-permute-start = (bf16[128,2048]{1,0:T(8,128)(2,1)S(1)}, bf16[128,2048]{1,0:T(8,128)(2,1)S(1)}, u32[]{:S(2)}, u32[]{:S(2)}) collective-permute-start(bf16[128,2048]{1,0:T(8,128)(2,1)S(1)} %fusion.1), channel_id=1, source_target_pairs={{0,16},{16,0},{1,17},{17,1},{2,18},{18,2},{3,19},{19,3},{4,20},{20... | collective-permute-start | bytes 1572872 | tf_op jit(solution)/shard_map/ppermute | solution.py:67
  27.6 22.7 %collective-permute-start.2 = (bf16[128,2048]{1,0:T(8,128)(2,1)S(1)}, bf16[128,2048]{1,0:T(8,128)(2,1)S(1)}, u32[]{:S(2)}, u32[]{:S(2)}) collective-permute-start(bf16[128,2048]{1,0:T(8,128)(2,1)S(1)} %fusion.1), channel_id=1, source_target_pairs={{0,8},{8,0},{1,9},{9,1},{2,10},{10,2},{3,11},{11,3},{4,12},{12,4},... | collective-permute-start | bytes 1572872 | tf_op jit(solution)/shard_map/ppermute | solution.py:68
  45.8 4.7 %collective-permute-start.1 = (bf16[128,2048]{1,0:T(8,128)(2,1)S(1)}, bf16[128,2048]{1,0:T(8,128)(2,1)S(1)}, u32[]{:S(2)}, u32[]{:S(2)}) collective-permute-start(bf16[128,2048]{1,0:T(8,128)(2,1)S(1)} %collective-permute-done), channel_id=1, source_target_pairs={{0,8},{8,0},{1,9},{9,1},{2,10},{10,2},{3,11},{11,3},{4,12},{12,4},... | collective-permute-start | bytes 1572872 | tf_op jit(solution)/shard_map/ppermute | solution.py:68
  50.6 21.8 %copy-start.2 = (bf16[1,1,16,512]{3,2,1,0:T(8,128)(2,1)S(1)}, bf16[1,1,16,512]{3,2,1,0:T(8,128)(2,1)}, u32[]{:S(2)}) copy-start(bf16[1,1,16,512]{3,2,1,0:T(8,128)(2,1)} %param.9) | copy-start | bytes 49156
  74.3 17.6 %all-to-all-start.2 = ((bf16[32,16,384]{2,1,0:T(8,128)(2,1)}), bf16[32,16,384]{2,1,0:T(8,128)(2,1)S(1)}, u32[]{:S(2)}, u32[]{:S(2)}) async-start(bf16[32,16,384]{2,1,0:T(8,128)(2,1)} %bitcast.25), calls=%async_computation.2 | async-start | bytes 786432 | tf_op jit(solution)/shard_map/all_to_all | solution.py:104
  135.5 16.2 %all-to-all-start.4 = ((f32[64,1,512]{2,1,0:T(1,128)}), f32[64,1,512]{2,1,0:T(1,128)S(1)}, u32[]{:S(2)}, u32[]{:S(2)}) async-start(f32[64,1,512]{2,1,0:T(1,128)} %broadcast_in_dim.45), calls=%async_computation.4 | async-start | bytes 262144 | tf_op jit(solution)/shard_map/all_to_all | solution.py:126

commit v2 on v1

--- a/solution.py
+++ b/solution.py
@@ -3,9 +3,8 @@
 from jax import lax
 from jax.sharding import Mesh, PartitionSpec as P
 
-ROW = ("y", "xh", "xl", "core")
-CHIPS = ("y", "xh", "xl")
-GROUP = ("xl", "core")
+ROW = ("yh", "yl", "xh", "xl", "core")
+CUBE = ("yl", "xl", "core")
 TEAM = ("xl", "core", "z")
 SWAP = [(0, 1), (1, 0)]
 MEMBERS = 4
@@ -51,7 +50,7 @@
     node_rows, width = features.shape[2], features.shape[3]
     rows = lax.axis_size(ROW)
     depth = lax.axis_size("z")
-    chips = lax.axis_size(CHIPS)
+    cube = lax.axis_size(CUBE)
     part = width // MEMBERS
     col_nodes = rows * node_rows
     block_rows = tile_mask.shape[3]
@@ -114,25 +113,26 @@
     )
     term = term.reshape(per_lane, share, part)
     term = lax.dynamic_index_in_dim(term, lax.axis_index("z") % per_lane, 0, keepdims=False)
-    extra = 8
-    term = jnp.broadcast_to(
-        term.astype(bf16)[:, None, None, :], (chips, rows // chips, extra, part)
-    ).reshape(rows, extra, part)
+    extra = share // cube
+    term = term.astype(bf16).reshape(1, 2, 1, MEMBERS, extra, part)
+    term = jnp.broadcast_to(term, (rows // (8 * MEMBERS), 2, 4, MEMBERS, extra, part))
+    term = term.reshape(rows, extra, part)
     out = lax.all_to_all(jnp.concatenate([grad, term], axis=1), ROW, 0, 0)
     out = out.reshape(rows // MEMBERS, MEMBERS, node_rows + extra, part)
     total = jnp.sum(out[:, :, :node_rows].astype(f32), axis=0)
     feature_grad = jnp.concatenate([total[m] for m in range(MEMBERS)], axis=1).astype(bf16)
-    weight_row = jnp.sum(out[:, :, node_rows].astype(f32), axis=0).reshape(1, 1, width)
-    weight_grad = lax.all_to_all(jnp.broadcast_to(weight_row, (chips, 1, width)), CHIPS, 0, 0)
+    weight_rows = jnp.sum(out[:, :, node_rows:].astype(f32), axis=0)
+    weight_rows = jnp.concatenate([weight_rows[m] for m in range(MEMBERS)], axis=1)
+    weight_grad = lax.all_to_all(jnp.broadcast_to(weight_rows[None], (cube, extra, width)), CUBE, 0, 0)
     return (
         activated.reshape(1, 1, node_rows, width),
         feature_grad.reshape(1, 1, node_rows, width),
-        weight_grad.reshape(chips, width),
+        weight_grad.reshape(share, width),
     )
 
 
 def solution(mesh):
-    fine = Mesh(mesh.devices.reshape(8, 4, 2, 2, 8), ("y", "xh", "xl", "core", "z"))
+    fine = Mesh(mesh.devices.reshape(4, 2, 4, 2, 2, 8), ROW + ("z",))
     in_specs = (
         P("z", ROW, None, None),
         P(),

time: 153 us -> 145 us (0.948)
  waiting for transfers between devices: 39.6 us -> 32.7 us
    all_to_all x1, waiting for transfers between devices: 10.9 us -> 3.99 us  [body(): lax.all_to_all(jnp.broadcast_to(weight_rows[None], (cube, extra, width)),...]
where the time goes in v2:
time: 145 us; the launch traced here: 144 us
  blocking collectives  62.1 us (43%)
  starting transfers between devices  36.1 us (25%)
  waiting for transfers between devices  32.7 us (23%)
  matrix products  6 us (4%)
  local copies, waits for them, and re-layouts  3.26 us (2%)
  other arithmetic  2.22 us (2%)
  between operations  1.67 us (1%)
    all_to_all x1, blocking collectives, body(): out = lax.all_to_all(jnp.concatenate([grad, term], axis=1), ROW, 0, 0)  40.7 us
    all_to_all x1, blocking collectives, body(): lax.all_to_all(partial, TEAM, 0, 0).reshape(MEMBERS, depth, node_rows, part)  21.3 us
    all_to_all x1, starting transfers between devices, body(): panels = lax.all_to_all(send.reshape(rows, node_rows, part), ROW, 0, 0)  19.4 us
    ppermute x1, waiting for transfers between devices, body(): across = lax.ppermute(dense, 'xl', SWAP)  15.7 us
    all_to_all x1, waiting for transfers between devices, body(): lax.all_to_all(both, TEAM, 0, 0)  12.9 us
    all_to_all x1, starting transfers between devices, body(): lax.all_to_all(both, TEAM, 0, 0)  4.66 us
    all_to_all x1, waiting for transfers between devices, body(): lax.all_to_all(jnp.broadcast_to(weight_rows[None], (cube, extra, width)),...  3.99 us
    all_to_all x1, starting transfers between devices, body(): lax.all_to_all(jnp.broadcast_to(weight_rows[None], (cube, extra, width)),...  3.32 us
  transfers between devices with their start and end apart: 6, of which 3 were waited for; matrix products, arithmetic and copies ran while one was open for 3% of the time, Pallas kernels for 0%

profile of v2, /device:TPU:1, one launch (start us, length us, event | category | flops | bytes accessed | tf_op | source)
XLA Modules:
  0.0 143.9 jit_solution(358858534017677912)
XLA Ops:
  0.7 0.8 reshape_squeeze.3
  1.5 0.9 broadcast_in_dim.10
  2.4 19.4 %all-to-all-start = ((bf16[128,16,128]{2,1,0:T(8,128)(2,1)}), bf16[128,16,128]{2,1,0:T(8,128)(2,1)S(1)}, u32[]{:S(2)}, u32[]{:S(2)}) async-start(bf16[128,16,128]{2,1,0:T(8,128)(2,1)} %bitcast.7), calls=%async_computation | async-start | bytes 1048576 | tf_op jit(solution)/shard_map/all_to_all | solution.py:60
  22.7 1.2 fusion.2
  23.8 0.4 fusion.1
  24.3 3.3 %collective-permute-start = (bf16[128,2048]{1,0:T(8,128)(2,1)S(1)}, bf16[128,2048]{1,0:T(8,128)(2,1)S(1)}, u32[]{:S(2)}, u32[]{:S(2)}) collective-permute-start(bf16[128,2048]{1,0:T(8,128)(2,1)S(1)} %fusion.1), channel_id=1, source_target_pairs={{0,16},{16,0},{1,17},{17,1},{2,18},{18,2},{3,19},{19,3},{4,20},{20... | collective-permute-start | bytes 1572872 | tf_op jit(solution)/shard_map/ppermute | solution.py:66
  27.6 2.5 %collective-permute-start.2 = (bf16[128,2048]{1,0:T(8,128)(2,1)S(1)}, bf16[128,2048]{1,0:T(8,128)(2,1)S(1)}, u32[]{:S(2)}, u32[]{:S(2)}) collective-permute-start(bf16[128,2048]{1,0:T(8,128)(2,1)S(1)} %fusion.1), channel_id=1, source_target_pairs={{0,8},{8,0},{1,9},{9,1},{2,10},{10,2},{3,11},{11,3},{4,12},{12,4},... | collective-permute-start | bytes 1572872 | tf_op jit(solution)/shard_map/ppermute | solution.py:67
  30.1 15.7 %collective-permute-done = bf16[128,2048]{1,0:T(8,128)(2,1)S(1)} collective-permute-done((bf16[128,2048]{1,0:T(8,128)(2,1)S(1)}, bf16[128,2048]{1,0:T(8,128)(2,1)S(1)}, u32[]{:S(2)}, u32[]{:S(2)}) %collective-permute-start) | collective-permute-done | bytes 524320 | tf_op jit(solution)/shard_map/ppermute | solution.py:66
  45.8 2.8 %collective-permute-start.1 = (bf16[128,2048]{1,0:T(8,128)(2,1)S(1)}, bf16[128,2048]{1,0:T(8,128)(2,1)S(1)}, u32[]{:S(2)}, u32[]{:S(2)}) collective-permute-start(bf16[128,2048]{1,0:T(8,128)(2,1)S(1)} %collective-permute-done), channel_id=1, source_target_pairs={{0,8},{8,0},{1,9},{9,1},{2,10},{10,2},{3,11},{11,3},{4,12},{12,4},... | collective-permute-start | bytes 1572872 | tf_op jit(solution)/shard_map/ppermute | solution.py:67
  48.6 1.3 convolution_convert_fusion
  50.0 0.3 convolution_convert_fusion.2
  50.3 0.3 convolution_convert_fusion.1
  50.6 0.3 select_bitcast_fusion.3
  50.9 21.3 %all_to_all.25 = bf16[32,16,128]{2,1,0:T(8,128)(2,1)S(1)} all-to-all(bf16[32,16,128]{2,1,0:T(8,128)(2,1)S(1)} %bitcast.115), channel_id=1, replica_groups=mesh['yh'=4,'yl'=2,'xh'=4,'xl'=2,'core'=2,'z'=8] {'xl','core','z'}, dimensions={0} | all-to-all | bytes 262144 | tf_op jit(solution)/shard_map/all_to_all | solution.py:71
  72.3 0.8 fusion.10
  73.2 0.2 convolution_convert_fusion.4
  73.5 0.8 pad_maximum_fusion.1
  74.3 4.7 %all-to-all-start.2 = ((bf16[32,16,384]{2,1,0:T(8,128)(2,1)}), bf16[32,16,384]{2,1,0:T(8,128)(2,1)S(1)}, u32[]{:S(2)}, u32[]{:S(2)}) async-start(bf16[32,16,384]{2,1,0:T(8,128)(2,1)} %bitcast.25), calls=%async_computation.2 | async-start | bytes 786432 | tf_op jit(solution)/shard_map/all_to_all | solution.py:103
  79.0 12.9 %all-to-all-done.2 = bf16[32,16,384]{2,1,0:T(8,128)(2,1)S(1)} async-done(((bf16[32,16,384]{2,1,0:T(8,128)(2,1)}), bf16[32,16,384]{2,1,0:T(8,128)(2,1)S(1)}, u32[]{:S(2)}, u32[]{:S(2)}) %all-to-all-start.2) | async-done | bytes 393248 | tf_op jit(solution)/shard_map/all_to_all | solution.py:103
  91.9 0.3 fusion.14
  92.3 0.2 fusion.7
  92.5 0.3 convolution_add_fusion.2
  92.9 0.3 convolution_add_fusion.1
  93.2 0.3 fusion
  93.6 0.1 pad_maximum_fusion
  93.8 40.7 %all_to_all.26 = bf16[128,24,128]{2,1,0:T(8,128)(2,1)S(1)} all-to-all(bf16[128,24,128]{2,1,0:T(8,128)(2,1)S(1)} %pad_maximum_fusion), channel_id=1, replica_groups=mesh['yh'=4,'yl'=2,'xh'=4,'xl'=2,'core'=2,'z'=8] {'yh','yl','xh','xl','c..., dimensions={0} | all-to-all | bytes 1572864 | tf_op jit(solution)/shard_map/all_to_all | solution.py:120
  134.6 0.1 slice_reduce_fusion
  134.7 0.7 broadcast_in_dim.14
  135.3 3.3 %all-to-all-start.4 = ((f32[8,8,512]{2,1,0:T(8,128)}), f32[8,8,512]{2,1,0:T(8,128)S(1)}, u32[]{:S(2)}, u32[]{:S(2)}) async-start(f32[8,8,512]{2,1,0:T(8,128)} %broadcast_in_dim.14), calls=%async_computation.4 | async-start | bytes 262144 | tf_op jit(solution)/shard_map/all_to_all | solution.py:126
  138.7 0.6 pad_maximum_fusion.4
  139.3 4.0 %all-to-all-done.4 = f32[8,8,512]{2,1,0:T(8,128)S(1)} async-done(((f32[8,8,512]{2,1,0:T(8,128)}), f32[8,8,512]{2,1,0:T(8,128)S(1)}, u32[]{:S(2)}, u32[]{:S(2)}) %all-to-all-start.4) | async-done | bytes 131104 | tf_op jit(solution)/shard_map/all_to_all | solution.py:126
  143.3 0.7 copy.29
  (37 shorter events, 0.4 us)
Async XLA Ops:
  0.6 71.7 %copy-start = (bf16[512,512]{1,0:T(8,128)(2,1)S(1)}, bf16[512,512]{1,0:T(8,128)(2,1)}, u32[]{:S(2)}) copy-start(bf16[512,512]{1,0:T(8,128)(2,1)} %param.8) | copy-start | bytes 1572868
  0.6 21.2 %copy-start.4 = (s32[1,128]{1,0:T(1,128)S(1)}, s32[1,128]{1,0:T(1,128)}, u32[]{:S(2)}) copy-start(s32[1,128]{1,0:T(1,128)} %param.13) | copy-start | bytes 1540
  0.7 21.2 %copy-start.1 = (s32[1,1,12,128,128]{4,3,2,1,0:T(8,128)S(1)}, s32[1,1,12,128,128]{4,3,2,1,0:T(8,128)}, u32[]{:S(2)}) copy-start(s32[1,1,12,128,128]{4,3,2,1,0:T(8,128)} %param.10) | copy-start | bytes 2359300
  2.4 20.2 %copy-start.3 = (s32[1,1,12]{2,1,0:T(1,128)S(1)}, s32[1,1,12]{2,1,0:T(1,128)}, u32[]{:S(2)}) copy-start(s32[1,1,12]{2,1,0:T(1,128)} %param.11) | copy-start | bytes 148
  2.4 46.2 %all-to-all-start = ((bf16[128,16,128]{2,1,0:T(8,128)(2,1)}), bf16[128,16,128]{2,1,0:T(8,128)(2,1)S(1)}, u32[]{:S(2)}, u32[]{:S(2)}) async-start(bf16[128,16,128]{2,1,0:T(8,128)(2,1)} %bitcast.7), calls=%async_computation | async-start | bytes 1048576 | tf_op jit(solution)/shard_map/all_to_all | solution.py:60
  24.3 21.6 %collective-permute-start = (bf16[128,2048]{1,0:T(8,128)(2,1)S(1)}, bf16[128,2048]{1,0:T(8,128)(2,1)S(1)}, u32[]{:S(2)}, u32[]{:S(2)}) collective-permute-start(bf16[128,2048]{1,0:T(8,128)(2,1)S(1)} %fusion.1), channel_id=1, source_target_pairs={{0,16},{16,0},{1,17},{17,1},{2,18},{18,2},{3,19},{19,3},{4,20},{20... | collective-permute-start | bytes 1572872 | tf_op jit(solution)/shard_map/ppermute | solution.py:66
  27.6 22.7 %collective-permute-start.2 = (bf16[128,2048]{1,0:T(8,128)(2,1)S(1)}, bf16[128,2048]{1,0:T(8,128)(2,1)S(1)}, u32[]{:S(2)}, u32[]{:S(2)}) collective-permute-start(bf16[128,2048]{1,0:T(8,128)(2,1)S(1)} %fusion.1), channel_id=1, source_target_pairs={{0,8},{8,0},{1,9},{9,1},{2,10},{10,2},{3,11},{11,3},{4,12},{12,4},... | collective-permute-start | bytes 1572872 | tf_op jit(solution)/shard_map/ppermute | solution.py:67
  45.8 4.7 %collective-permute-start.1 = (bf16[128,2048]{1,0:T(8,128)(2,1)S(1)}, bf16[128,2048]{1,0:T(8,128)(2,1)S(1)}, u32[]{:S(2)}, u32[]{:S(2)}) collective-permute-start(bf16[128,2048]{1,0:T(8,128)(2,1)S(1)} %collective-permute-done), channel_id=1, source_target_pairs={{0,8},{8,0},{1,9},{9,1},{2,10},{10,2},{3,11},{11,3},{4,12},{12,4},... | collective-permute-start | bytes 1572872 | tf_op jit(solution)/shard_map/ppermute | solution.py:67
  50.6 21.8 %copy-start.2 = (bf16[1,1,16,512]{3,2,1,0:T(8,128)(2,1)S(1)}, bf16[1,1,16,512]{3,2,1,0:T(8,128)(2,1)}, u32[]{:S(2)}) copy-start(bf16[1,1,16,512]{3,2,1,0:T(8,128)(2,1)} %param.9) | copy-start | bytes 49156
  74.3 17.6 %all-to-all-start.2 = ((bf16[32,16,384]{2,1,0:T(8,128)(2,1)}), bf16[32,16,384]{2,1,0:T(8,128)(2,1)S(1)}, u32[]{:S(2)}, u32[]{:S(2)}) async-start(bf16[32,16,384]{2,1,0:T(8,128)(2,1)} %bitcast.25), calls=%async_computation.2 | async-start | bytes 786432 | tf_op jit(solution)/shard_map/all_to_all | solution.py:103
  135.3 7.9 %all-to-all-start.4 = ((f32[8,8,512]{2,1,0:T(8,128)}), f32[8,8,512]{2,1,0:T(8,128)S(1)}, u32[]{:S(2)}, u32[]{:S(2)}) async-start(f32[8,8,512]{2,1,0:T(8,128)} %broadcast_in_dim.14), calls=%async_computation.4 | async-start | bytes 262144 | tf_op jit(solution)/shard_map/all_to_all | solution.py:126

commit v3 on v2

--- a/solution.py
+++ b/solution.py
@@ -1,6 +1,8 @@
 import jax
 import jax.numpy as jnp
 from jax import lax
+from jax.experimental import pallas as pl
+from jax.experimental.pallas import tpu as pltpu
 from jax.sharding import Mesh, PartitionSpec as P
 
 ROW = ("yh", "yl", "xh", "xl", "core")
@@ -8,11 +10,6 @@
 TEAM = ("xl", "core", "z")
 SWAP = [(0, 1), (1, 0)]
 MEMBERS = 4
-
-
-def slope_of(preact):
-    sigma = jax.nn.sigmoid(preact)
-    return sigma * (1.0 + preact * (1.0 - sigma))
 
 
 def exclusive(blocks):
@@ -33,16 +30,74 @@
     ]
 
 
-def dense_of(tile_mask, tile_cols, tile_count, degree, panel_count):
-    slots, block_rows, tile_width = tile_mask.shape
-    live = (jnp.arange(slots, dtype=jnp.int32) < tile_count).astype(jnp.float32)
-    onehot = (tile_cols[:, None] == jnp.arange(panel_count, dtype=jnp.int32)[None, :]).astype(
-        jnp.float32
-    )
-    onehot = onehot * live[:, None]
-    counts = jnp.einsum("kp,kit->ipt", onehot, tile_mask.astype(jnp.float32))
-    counts = counts.reshape(block_rows, panel_count * tile_width)
-    return (counts * lax.rsqrt(degree.astype(jnp.float32))[:, None]).astype(jnp.bfloat16)
+def local(kernel, out, ins, flops, moved, operands, scratch=()):
+    return pl.pallas_call(
+        kernel,
+        out_shape=out,
+        in_specs=[pl.BlockSpec(memory_space=space) for space in ins],
+        scratch_shapes=scratch,
+        cost_estimate=pl.CostEstimate(flops=flops, bytes_accessed=moved, transcendentals=0),
+        compiler_params=pltpu.CompilerParams(vmem_limit_bytes=32 * 2**20),
+    )(*operands)
+
+
+def spread_kernel(own_ref, out_ref):
+    groups, members, node_rows, part = out_ref.shape
+    for m in range(members):
+        quarter = own_ref[:, m * part : (m + 1) * part]
+        out_ref[:, m] = jnp.broadcast_to(quarter[None], (groups, node_rows, part))
+
+
+def compact_kernel(count_ref, cols_ref, scale_ref, mask_ref, out_ref):
+    slots, block_rows, tile_width = mask_ref.shape
+    scale = jnp.broadcast_to(scale_ref[...], (block_rows, block_rows)).T
+    count = count_ref[0]
+    for s in range(slots):
+        kept = scale * (s < count).astype(jnp.float32)
+        tile = mask_ref[s].astype(jnp.float32) * kept
+        out_ref[s * block_rows : (s + 1) * block_rows, :] = tile.astype(jnp.bfloat16)
+    tail = out_ref.shape[0] - slots * block_rows
+    row = lax.broadcasted_iota(jnp.int32, (tail, tile_width), 0)
+    place = jnp.zeros((tail, tile_width), jnp.int32)
+    for s in range(slots):
+        place = jnp.where(row == s, cols_ref[s], place)
+    out_ref[slots * block_rows :, :] = place.astype(jnp.float32).astype(jnp.bfloat16)
+
+
+def place_kernel(tiles_ref, out_ref):
+    block_rows = out_ref.shape[0]
+    tile_width = tiles_ref.shape[1]
+    slots = tiles_ref.shape[0] // block_rows
+    out_ref[...] = jnp.zeros_like(out_ref)
+    place = tiles_ref[slots * block_rows :, :].astype(jnp.float32)
+    for s in range(slots):
+        col = jnp.max(place[s : s + 1, :]).astype(jnp.int32)
+        start = pl.multiple_of(col * tile_width, tile_width)
+        out_ref[:, pl.ds(start, tile_width)] = tiles_ref[s * block_rows : (s + 1) * block_rows, :]
+
+
+def node_kernel(sums_ref, weight_ref, cotangent_ref, active_ref, out_ref):
+    f32, bf16 = jnp.float32, jnp.bfloat16
+    members, depth, node_rows, part = sums_ref.shape
+    width = members * part
+    lanes = out_ref.shape[2] - 2 * part
+    sums = [jnp.sum(sums_ref[m].astype(f32), axis=0).astype(bf16) for m in range(members)]
+    own_inputs = jnp.concatenate(sums, axis=1)
+    pre = jnp.dot(own_inputs, weight_ref[...], preferred_element_type=f32)
+    sigma = 1.0 / (1.0 + jnp.exp(-pre))
+    active_ref[...] = (pre * sigma).astype(bf16)
+    slope = cotangent_ref[...].astype(f32) * (sigma * (1.0 + pre * (1.0 - sigma)))
+    slope = slope.astype(bf16)
+    proj = lax.dot_general(
+        slope, weight_ref[...], (((1,), (1,)), ((), ())), preferred_element_type=f32
+    ).astype(bf16)
+    for m in range(members):
+        for d in range(depth):
+            first = d * (width // depth) // lanes * lanes
+            at = m * depth + d
+            out_ref[at, :, :part] = proj[:, m * part : (m + 1) * part]
+            out_ref[at, :, part : 2 * part] = slope[:, m * part : (m + 1) * part]
+            out_ref[at, :, 2 * part :] = own_inputs[:, first : first + lanes]
 
 
 def body(features, weight, cotangent, tile_mask, tile_cols, tile_count, degree):
@@ -55,51 +110,57 @@
     col_nodes = rows * node_rows
     block_rows = tile_mask.shape[3]
 
-    own = features[0, 0].reshape(node_rows, MEMBERS, part).transpose(1, 0, 2)
-    send = jnp.broadcast_to(own[None], (rows // MEMBERS, MEMBERS, node_rows, part))
+    vmem, smem = pltpu.VMEM, pltpu.SMEM
+    send = local(
+        spread_kernel,
+        jax.ShapeDtypeStruct((rows // MEMBERS, MEMBERS, node_rows, part), bf16),
+        [vmem],
+        0,
+        2 * col_nodes * part,
+        [features[0, 0]],
+    )
     panels = lax.all_to_all(send.reshape(rows, node_rows, part), ROW, 0, 0)
     panels = panels.reshape(col_nodes, part)
 
-    dense = dense_of(
-        tile_mask[0, 0], tile_cols[0, 0], tile_count[0, 0], degree[0], col_nodes // tile_mask.shape[4]
-    )
-    across = lax.ppermute(dense, "xl", SWAP)
-    blocks = [dense, lax.ppermute(dense, "core", SWAP), across, lax.ppermute(across, "core", SWAP)]
+    slots, tile_width = tile_mask.shape[2], tile_mask.shape[4]
+    tiles = local(
+        compact_kernel,
+        jax.ShapeDtypeStruct((slots * block_rows + 16, tile_width), bf16),
+        [smem, smem, vmem, vmem],
+        2 * slots * block_rows * tile_width,
+        6 * slots * block_rows * tile_width,
+        [tile_count[0], tile_cols[0, 0], lax.rsqrt(degree.astype(f32)), tile_mask[0, 0]],
+    )
+    across = lax.ppermute(tiles, "xl", SWAP)
+    blocks = [
+        local(
+            place_kernel,
+            jax.ShapeDtypeStruct((block_rows, col_nodes), bf16),
+            [vmem],
+            0,
+            2 * (slots + 2 * col_nodes // tile_width) * block_rows * tile_width,
+            [block],
+        )
+        for block in (tiles, lax.ppermute(tiles, "core", SWAP), across, lax.ppermute(across, "core", SWAP))
+    ]
 
     partial = [jnp.dot(b, panels, preferred_element_type=f32).astype(bf16) for b in blocks]
     partial = jnp.stack(exclusive(partial)).reshape(MEMBERS * depth, node_rows, part)
     sums = lax.all_to_all(partial, TEAM, 0, 0).reshape(MEMBERS, depth, node_rows, part)
-    sums = jnp.sum(sums.astype(f32), axis=1)
-    own_inputs = jnp.concatenate([sums[m] for m in range(MEMBERS)], axis=1).astype(bf16)
-
-    own_pre = jnp.dot(own_inputs, weight, preferred_element_type=f32)
-    activated = jax.nn.silu(own_pre).astype(bf16)
-    own_slope = (cotangent[0, 0].astype(f32) * slope_of(own_pre)).astype(bf16)
-    own_proj = lax.dot_general(
-        own_slope, weight, (((1,), (1,)), ((), ())), preferred_element_type=f32
-    ).astype(bf16)
-
     lanes = 128
     share = width // depth
     per_lane = lanes // share
-    quarters = jnp.stack(
-        [
-            jnp.concatenate(
-                [own_proj[:, m * part : (m + 1) * part], own_slope[:, m * part : (m + 1) * part]], axis=1
-            )
-            for m in range(MEMBERS)
-        ]
-    )
-    slices = jnp.stack(
-        [own_inputs[:, (d // per_lane) * lanes : (d // per_lane + 1) * lanes] for d in range(depth)]
-    )
-    both = jnp.concatenate(
-        [
-            jnp.broadcast_to(quarters[:, None], (MEMBERS, depth, node_rows, 2 * part)),
-            jnp.broadcast_to(slices[None], (MEMBERS, depth, node_rows, lanes)),
-        ],
-        axis=3,
-    ).reshape(MEMBERS * depth, node_rows, 2 * part + lanes)
+    activated, both = local(
+        node_kernel,
+        (
+            jax.ShapeDtypeStruct((node_rows, width), bf16),
+            jax.ShapeDtypeStruct((MEMBERS * depth, node_rows, 2 * part + lanes), bf16),
+        ),
+        [vmem, vmem, vmem],
+        4 * node_rows * width * width,
+        2 * width * width + 8 * col_nodes * part,
+        [sums, weight, cotangent[0, 0]],
+    )
     both = lax.all_to_all(both, TEAM, 0, 0).reshape(MEMBERS * block_rows, 2 * part + lanes)
     proj = exclusive(both[:, :part].reshape(MEMBERS, block_rows, part))
     contract_rows = (((0,), (0,)), ((), ()))

time: 145 us -> 142 us (0.979)
  Pallas kernels: 0 us -> 3.59 us
  matrix products: 6 us -> 2.76 us
    pallas_call x0 -> x7, Pallas kernels: none -> 3.59 us  [local(): pl.pallas_call(kernel, out_shape=out, in_specs=[pl.BlockSpec(memory_space...]
    dot_general x3 -> x0, matrix products: 2.22 us -> none  [the longest x1 1.17 us: dense_of(): counts = jnp.einsum('kp,kit->ipt', onehot, tile_mask.astype(jnp.float32))]
    ppermute x2, waiting for transfers between devices: 15.7 us -> 14 us  [the longest x1 14 us: body(): across = lax.ppermute(tiles, 'xl', SWAP)]
  transfers between devices with their start and end apart: 6 -> 6, of which waited for: 3 -> 4; matrix products, arithmetic and copies ran while one was open for 3% -> 0% of each run, Pallas kernels for 0% -> 1%
where the time goes in v3:
time: 142 us; the launch traced here: 141 us
  blocking collectives  62.4 us (44%)
  starting transfers between devices  35.9 us (25%)
  waiting for transfers between devices  31.6 us (22%)
  Pallas kernels  3.59 us (3%)
  matrix products  2.76 us (2%)
  local copies, waits for them, and re-layouts  2.18 us (2%)
  between operations  1.59 us (1%)
    all_to_all x1, blocking collectives, body(): out = lax.all_to_all(jnp.concatenate([grad, term], axis=1), ROW, 0, 0)  40.8 us
    all_to_all x1, blocking collectives, body(): lax.all_to_all(partial, TEAM, 0, 0).reshape(MEMBERS, depth, node_rows, part)  21.6 us
    all_to_all x1, starting transfers between devices, body(): panels = lax.all_to_all(send.reshape(rows, node_rows, part), ROW, 0, 0)  19.3 us
    ppermute x1, waiting for transfers between devices, body(): across = lax.ppermute(tiles, 'xl', SWAP)  14 us
    all_to_all x1, waiting for transfers between devices, body(): lax.all_to_all(both, TEAM, 0, 0)  12.9 us
    all_to_all x1, starting transfers between devices, body(): lax.all_to_all(both, TEAM, 0, 0)  4.67 us
    all_to_all x1, waiting for transfers between devices, body(): lax.all_to_all(jnp.broadcast_to(weight_rows[None], (cube, extra, width)),...  3.99 us
    pallas_call x7, Pallas kernels, local(): pl.pallas_call(kernel, out_shape=out, in_specs=[pl.BlockSpec(memory_space...  3.59 us
  transfers between devices with their start and end apart: 6, of which 4 were waited for; matrix products, arithmetic and copies ran while one was open for 0% of the time, Pallas kernels for 1%

profile of v3, /device:TPU:1, one launch (start us, length us, event | category | flops | bytes accessed | tf_op | source)
XLA Modules:
  0.0 140.9 jit_solution(1472635096863998960)
XLA Ops:
  0.7 0.8 copy-done.2
  1.4 0.9 shard_map.96
  2.4 19.3 %all-to-all-start = ((bf16[128,16,128]{2,1,0:T(8,128)(2,1)}), bf16[128,16,128]{2,1,0:T(8,128)(2,1)S(1)}, u32[]{:S(2)}, u32[]{:S(2)}) async-start(bf16[128,16,128]{2,1,0:T(8,128)(2,1)} %bitcast.4), calls=%async_computation | async-start | bytes 1048576 | tf_op jit(solution)/shard_map/all_to_all | solution.py:122
  22.4 0.7 shard_map.94.tiles_ref
  23.1 3.3 %collective-permute-start = (bf16[1552,128]{1,0:T(8,128)(2,1)S(1)}, bf16[1552,128]{1,0:T(8,128)(2,1)S(1)}, u32[]{:S(2)}, u32[]{:S(2)}) collective-permute-start(bf16[1552,128]{1,0:T(8,128)(2,1)S(1)} %shard_map.94.tiles_ref), channel_id=1, source_target_pairs={{0,16},{16,0},{1,17},{17,1},{2,18},{18,2},{3,19},{19,3},{4,20},{20... | collective-permute-start | bytes 1191944 | tf_op jit(solution)/shard_map/ppermute | solution.py:134
  26.4 2.5 %collective-permute-start.2 = (bf16[1552,128]{1,0:T(8,128)(2,1)S(1)}, bf16[1552,128]{1,0:T(8,128)(2,1)S(1)}, u32[]{:S(2)}, u32[]{:S(2)}) collective-permute-start(bf16[1552,128]{1,0:T(8,128)(2,1)S(1)} %shard_map.94.tiles_ref), channel_id=1, source_target_pairs={{0,8},{8,0},{1,9},{9,1},{2,10},{10,2},{3,11},{11,3},{4,12},{12,4},... | collective-permute-start | bytes 1191944 | tf_op jit(solution)/shard_map/ppermute | solution.py:144
  28.9 14.0 %collective-permute-done.tiles_ref = bf16[1552,128]{1,0:T(8,128)(2,1)S(1)} collective-permute-done((bf16[1552,128]{1,0:T(8,128)(2,1)S(1)}, bf16[1552,128]{1,0:T(8,128)(2,1)S(1)}, u32[]{:S(2)}, u32[]{:S(2)}) %collective-permute-start) | collective-permute-done | bytes 397344 | tf_op jit(solution)/shard_map/ppermute | solution.py:134
  42.9 2.8 %collective-permute-start.1 = (bf16[1552,128]{1,0:T(8,128)(2,1)S(1)}, bf16[1552,128]{1,0:T(8,128)(2,1)S(1)}, u32[]{:S(2)}, u32[]{:S(2)}) collective-permute-start(bf16[1552,128]{1,0:T(8,128)(2,1)S(1)} %collective-permute-done.tiles_ref), channel_id=1, source_target_pairs={{0,8},{8,0},{1,9},{9,1},{2,10},{10,2},{3,11},{11,3},{4,12},{12,4},... | collective-permute-start | bytes 1191944 | tf_op jit(solution)/shard_map/ppermute | solution.py:144
  45.7 0.2 shard_map.99
  45.9 0.2 shard_map.97
  46.1 0.2 shard_map.98
  46.4 0.7 collective-permute-done.1.tiles_ref
  47.0 0.2 shard_map.95
  47.3 0.3 convolution_convert_fusion.2
  47.6 0.3 convolution_convert_fusion.1
  47.9 0.3 convolution_convert_fusion
  48.2 0.3 select_bitcast_fusion.3
  48.5 21.6 %all_to_all.25 = bf16[32,16,128]{2,1,0:T(8,128)(2,1)S(1)} all-to-all(bf16[32,16,128]{2,1,0:T(8,128)(2,1)S(1)} %bitcast.73), channel_id=1, replica_groups=mesh['yh'=4,'yl'=2,'xh'=4,'xl'=2,'core'=2,'z'=8] {'xl','core','z'}, dimensions={0} | all-to-all | bytes 262144 | tf_op jit(solution)/shard_map/all_to_all | solution.py:149
  70.1 1.1 shard_map.100
  71.3 4.7 %all-to-all-start.2 = ((bf16[32,16,384]{2,1,0:T(8,128)(2,1)}), bf16[32,16,384]{2,1,0:T(8,128)(2,1)S(1)}, u32[]{:S(2)}, u32[]{:S(2)}) async-start(bf16[32,16,384]{2,1,0:T(8,128)(2,1)} %get-tuple-element.6), calls=%async_computation.2 | async-start | bytes 786432 | tf_op jit(solution)/shard_map/all_to_all | solution.py:164
  75.9 12.9 %all-to-all-done.2 = bf16[32,16,384]{2,1,0:T(8,128)(2,1)S(1)} async-done(((bf16[32,16,384]{2,1,0:T(8,128)(2,1)}), bf16[32,16,384]{2,1,0:T(8,128)(2,1)S(1)}, u32[]{:S(2)}, u32[]{:S(2)}) %all-to-all-start.2) | async-done | bytes 393248 | tf_op jit(solution)/shard_map/all_to_all | solution.py:164
  88.9 0.3 fusion.7
  89.2 0.2 fusion.1
  89.5 0.3 convolution_add_fusion.2
  89.8 0.3 convolution_add_fusion.1
  90.2 0.3 fusion
  90.7 40.8 %all_to_all.26 = bf16[128,24,128]{2,1,0:T(8,128)(2,1)S(1)} all-to-all(bf16[128,24,128]{2,1,0:T(8,128)(2,1)S(1)} %pad_maximum_fusion), channel_id=1, replica_groups=mesh['yh'=4,'yl'=2,'xh'=4,'xl'=2,'core'=2,'z'=8] {'yh','yl','xh','xl','c..., dimensions={0} | all-to-all | bytes 1572864 | tf_op jit(solution)/shard_map/all_to_all | solution.py:181
  131.6 0.7 broadcast_in_dim.5
  132.3 3.3 %all-to-all-start.4 = ((f32[8,8,512]{2,1,0:T(8,128)}), f32[8,8,512]{2,1,0:T(8,128)S(1)}, u32[]{:S(2)}, u32[]{:S(2)}) async-start(f32[8,8,512]{2,1,0:T(8,128)} %broadcast_in_dim.5), calls=%async_computation.4 | async-start | bytes 262144 | tf_op jit(solution)/shard_map/all_to_all | solution.py:187
  135.7 0.6 pad_maximum_fusion.2
  136.3 4.0 %all-to-all-done.4 = f32[8,8,512]{2,1,0:T(8,128)S(1)} async-done(((f32[8,8,512]{2,1,0:T(8,128)}), f32[8,8,512]{2,1,0:T(8,128)S(1)}, u32[]{:S(2)}, u32[]{:S(2)}) %all-to-all-start.4) | async-done | bytes 131104 | tf_op jit(solution)/shard_map/all_to_all | solution.py:187
  140.3 0.7 copy.12
  (23 shorter events, 0.4 us)
Async XLA Ops:
  0.6 21.7 %copy-start = (s32[1,1,12,128,128]{4,3,2,1,0:T(8,128)S(1)}, s32[1,1,12,128,128]{4,3,2,1,0:T(8,128)}, u32[]{:S(2)}) copy-start(s32[1,1,12,128,128]{4,3,2,1,0:T(8,128)} %param.10) | copy-start | bytes 2359300
  0.6 0.8 copy-start.2
  1.4 20.9 %copy-start.5 = (s32[1,128]{1,0:T(1,128)S(1)}, s32[1,128]{1,0:T(1,128)}, u32[]{:S(2)}) copy-start(s32[1,128]{1,0:T(1,128)} %param.13) | copy-start | bytes 1540
  1.4 20.9 %copy-start.4 = (s32[1,1,12]{2,1,0:T(1,128)S(1)}, s32[1,1,12]{2,1,0:T(1,128)}, u32[]{:S(2)}) copy-start(s32[1,1,12]{2,1,0:T(1,128)} %param.11) | copy-start | bytes 148
  2.4 44.9 %all-to-all-start = ((bf16[128,16,128]{2,1,0:T(8,128)(2,1)}), bf16[128,16,128]{2,1,0:T(8,128)(2,1)S(1)}, u32[]{:S(2)}, u32[]{:S(2)}) async-start(bf16[128,16,128]{2,1,0:T(8,128)(2,1)} %bitcast.4), calls=%async_computation | async-start | bytes 1048576 | tf_op jit(solution)/shard_map/all_to_all | solution.py:122
  23.1 19.8 %collective-permute-start = (bf16[1552,128]{1,0:T(8,128)(2,1)S(1)}, bf16[1552,128]{1,0:T(8,128)(2,1)S(1)}, u32[]{:S(2)}, u32[]{:S(2)}) collective-permute-start(bf16[1552,128]{1,0:T(8,128)(2,1)S(1)} %shard_map.94.tiles_ref), channel_id=1, source_target_pairs={{0,16},{16,0},{1,17},{17,1},{2,18},{18,2},{3,19},{19,3},{4,20},{20... | collective-permute-start | bytes 1191944 | tf_op jit(solution)/shard_map/ppermute | solution.py:134
  26.4 19.8 %collective-permute-start.2 = (bf16[1552,128]{1,0:T(8,128)(2,1)S(1)}, bf16[1552,128]{1,0:T(8,128)(2,1)S(1)}, u32[]{:S(2)}, u32[]{:S(2)}) collective-permute-start(bf16[1552,128]{1,0:T(8,128)(2,1)S(1)} %shard_map.94.tiles_ref), channel_id=1, source_target_pairs={{0,8},{8,0},{1,9},{9,1},{2,10},{10,2},{3,11},{11,3},{4,12},{12,4},... | collective-permute-start | bytes 1191944 | tf_op jit(solution)/shard_map/ppermute | solution.py:144
  42.9 4.1 %collective-permute-start.1 = (bf16[1552,128]{1,0:T(8,128)(2,1)S(1)}, bf16[1552,128]{1,0:T(8,128)(2,1)S(1)}, u32[]{:S(2)}, u32[]{:S(2)}) collective-permute-start(bf16[1552,128]{1,0:T(8,128)(2,1)S(1)} %collective-permute-done.tiles_ref), channel_id=1, source_target_pairs={{0,8},{8,0},{1,9},{9,1},{2,10},{10,2},{3,11},{11,3},{4,12},{12,4},... | collective-permute-start | bytes 1191944 | tf_op jit(solution)/shard_map/ppermute | solution.py:144
  48.2 21.9 %copy-start.1 = (bf16[512,512]{1,0:T(8,128)(2,1)S(1)}, bf16[512,512]{1,0:T(8,128)(2,1)}, u32[]{:S(2)}) copy-start(bf16[512,512]{1,0:T(8,128)(2,1)} %weight_ref.1) | copy-start | bytes 1572868
  48.2 21.9 %copy-start.3 = (bf16[1,1,16,512]{3,2,1,0:T(8,128)(2,1)S(1)}, bf16[1,1,16,512]{3,2,1,0:T(8,128)(2,1)}, u32[]{:S(2)}) copy-start(bf16[1,1,16,512]{3,2,1,0:T(8,128)(2,1)} %param.9) | copy-start | bytes 49156
  71.3 17.6 %all-to-all-start.2 = ((bf16[32,16,384]{2,1,0:T(8,128)(2,1)}), bf16[32,16,384]{2,1,0:T(8,128)(2,1)S(1)}, u32[]{:S(2)}, u32[]{:S(2)}) async-start(bf16[32,16,384]{2,1,0:T(8,128)(2,1)} %get-tuple-element.6), calls=%async_computation.2 | async-start | bytes 786432 | tf_op jit(solution)/shard_map/all_to_all | solution.py:164
  132.3 7.9 %all-to-all-start.4 = ((f32[8,8,512]{2,1,0:T(8,128)}), f32[8,8,512]{2,1,0:T(8,128)S(1)}, u32[]{:S(2)}, u32[]{:S(2)}) async-start(f32[8,8,512]{2,1,0:T(8,128)} %broadcast_in_dim.5), calls=%async_computation.4 | async-start | bytes 262144 | tf_op jit(solution)/shard_map/all_to_all | solution.py:187

commit v4 on v3

--- a/solution.py
+++ b/solution.py
@@ -80,7 +80,10 @@
     f32, bf16 = jnp.float32, jnp.bfloat16
     members, depth, node_rows, part = sums_ref.shape
     width = members * part
-    lanes = out_ref.shape[2] - 2 * part
+    lanes = out_ref.shape[2]
+    share = width // depth
+    few = node_rows // 2
+    left = lax.broadcasted_iota(jnp.int32, (few, lanes), 1) < share
     sums = [jnp.sum(sums_ref[m].astype(f32), axis=0).astype(bf16) for m in range(members)]
     own_inputs = jnp.concatenate(sums, axis=1)
     pre = jnp.dot(own_inputs, weight_ref[...], preferred_element_type=f32)
@@ -91,13 +94,22 @@
     proj = lax.dot_general(
         slope, weight_ref[...], (((1,), (1,)), ((), ())), preferred_element_type=f32
     ).astype(bf16)
+    packed = []
+    for d in range(depth):
+        first = d * share // lanes * lanes
+        both = own_inputs[:, first : first + lanes].astype(f32)
+        early, late = both[:few], both[few:]
+        if d * share == first:
+            pair = jnp.where(left, early, pltpu.roll(late, share, 1))
+        else:
+            pair = jnp.where(left, pltpu.roll(early, share, 1), late)
+        packed.append(pair.astype(bf16))
     for m in range(members):
         for d in range(depth):
-            first = d * (width // depth) // lanes * lanes
             at = m * depth + d
-            out_ref[at, :, :part] = proj[:, m * part : (m + 1) * part]
-            out_ref[at, :, part : 2 * part] = slope[:, m * part : (m + 1) * part]
-            out_ref[at, :, 2 * part :] = own_inputs[:, first : first + lanes]
+            out_ref[at, :node_rows] = proj[:, m * part : (m + 1) * part]
+            out_ref[at, node_rows : 2 * node_rows] = slope[:, m * part : (m + 1) * part]
+            out_ref[at, 2 * node_rows :] = packed[d]
 
 
 def body(features, weight, cotangent, tile_mask, tile_cols, tile_count, degree):
@@ -147,33 +159,33 @@
     partial = [jnp.dot(b, panels, preferred_element_type=f32).astype(bf16) for b in blocks]
     partial = jnp.stack(exclusive(partial)).reshape(MEMBERS * depth, node_rows, part)
     sums = lax.all_to_all(partial, TEAM, 0, 0).reshape(MEMBERS, depth, node_rows, part)
-    lanes = 128
     share = width // depth
-    per_lane = lanes // share
+    few = node_rows // 2
+    tall = 2 * node_rows + few
     activated, both = local(
         node_kernel,
         (
             jax.ShapeDtypeStruct((node_rows, width), bf16),
-            jax.ShapeDtypeStruct((MEMBERS * depth, node_rows, 2 * part + lanes), bf16),
+            jax.ShapeDtypeStruct((MEMBERS * depth, tall, part), bf16),
         ),
         [vmem, vmem, vmem],
         4 * node_rows * width * width,
         2 * width * width + 8 * col_nodes * part,
         [sums, weight, cotangent[0, 0]],
     )
-    both = lax.all_to_all(both, TEAM, 0, 0).reshape(MEMBERS * block_rows, 2 * part + lanes)
-    proj = exclusive(both[:, :part].reshape(MEMBERS, block_rows, part))
+    both = lax.all_to_all(both, TEAM, 0, 0)
+    proj = exclusive(both[:, :node_rows].reshape(MEMBERS, block_rows, part))
     contract_rows = (((0,), (0,)), ((), ()))
     grad = sum(
         lax.dot_general(b, p, contract_rows, preferred_element_type=f32)
         for b, p in zip(blocks, proj, strict=True)
     )
     grad = grad.astype(bf16).reshape(rows, node_rows, part)
-    term = lax.dot_general(
-        both[:, 2 * part :], both[:, part : 2 * part], contract_rows, preferred_element_type=f32
-    )
-    term = term.reshape(per_lane, share, part)
-    term = lax.dynamic_index_in_dim(term, lax.axis_index("z") % per_lane, 0, keepdims=False)
+    slope = both[:, node_rows : 2 * node_rows].reshape(-1, 2, few, part)
+    slope = jnp.concatenate([slope[:, 0], slope[:, 1]], axis=2).reshape(-1, 2 * part)
+    packed = both[:, 2 * node_rows :].reshape(-1, part)
+    term = lax.dot_general(packed, slope, contract_rows, preferred_element_type=f32)
+    term = term[:share, :part] + term[share:, part:]
     extra = share // cube
     term = term.astype(bf16).reshape(1, 2, 1, MEMBERS, extra, part)
     term = jnp.broadcast_to(term, (rows // (8 * MEMBERS), 2, 4, MEMBERS, extra, part))

time: 142 us -> 144 us (1.014)
  blocking collectives: 62.4 us -> 77.4 us
  waiting for transfers between devices: 31.6 us -> 18.2 us
  matrix products: 2.76 us -> 6.94 us
  starting transfers between devices: 35.9 us -> 32.3 us
    all_to_all x0 -> x1, blocking collectives: none -> 15.8 us  [body(): both = lax.all_to_all(both, TEAM, 0, 0)]
    all_to_all x1 -> x0, waiting for transfers between devices: 12.9 us -> none  [body(): lax.all_to_all(both, TEAM, 0, 0)]
    all_to_all x1 -> x0, starting transfers between devices: 4.67 us -> none  [body(): lax.all_to_all(both, TEAM, 0, 0)]
    dot_general x4, matrix products: 1.19 us -> 5.37 us  [body(): jnp.dot(b, panels, preferred_element_type=f32).astype(bf16)]
  transfers between devices with their start and end apart: 6 -> 5, of which waited for: 4 -> 3; matrix products, arithmetic and copies ran while one was open for 0% -> 0% of each run, Pallas kernels for 1% -> 1%
where the time goes in v4:
time: 144 us; the launch traced here: 143 us
  blocking collectives  77.4 us (54%)
  starting transfers between devices  32.3 us (22%)
  waiting for transfers between devices  18.2 us (13%)
  matrix products  6.94 us (5%)
  Pallas kernels  3.26 us (2%)
  local copies, waits for them, and re-layouts  2.21 us (2%)
  between operations  1.6 us (1%)
    all_to_all x1, blocking collectives, body(): out = lax.all_to_all(jnp.concatenate([grad, term], axis=1), ROW, 0, 0)  40.6 us
    all_to_all x1, blocking collectives, body(): lax.all_to_all(partial, TEAM, 0, 0).reshape(MEMBERS, depth, node_rows, part)  21 us
    all_to_all x1, starting transfers between devices, body(): panels = lax.all_to_all(send.reshape(rows, node_rows, part), ROW, 0, 0)  20.4 us
    all_to_all x1, blocking collectives, body(): both = lax.all_to_all(both, TEAM, 0, 0)  15.8 us
    ppermute x1, waiting for transfers between devices, body(): across = lax.ppermute(tiles, 'xl', SWAP)  13.5 us
    dot_general x4, matrix products, body(): jnp.dot(b, panels, preferred_element_type=f32).astype(bf16)  5.37 us
    all_to_all x1, waiting for transfers between devices, body(): lax.all_to_all(jnp.broadcast_to(weight_rows[None], (cube, extra, width)),...  3.99 us
    all_to_all x1, starting transfers between devices, body(): lax.all_to_all(jnp.broadcast_to(weight_rows[None], (cube, extra, width)),...  3.32 us
  transfers between devices with their start and end apart: 5, of which 3 were waited for; matrix products, arithmetic and copies ran while one was open for 0% of the time, Pallas kernels for 1%

profile of v4, /device:TPU:1, one launch (start us, length us, event | category | flops | bytes accessed | tf_op | source)
XLA Modules:
  0.0 142.9 jit_solution(8675171024871893783)
XLA Ops:
  0.7 0.8 copy-done.2
  1.4 0.9 shard_map.96
  2.4 20.4 %all-to-all-start = ((bf16[128,16,128]{2,1,0:T(8,128)(2,1)}), bf16[128,16,128]{2,1,0:T(8,128)(2,1)}, u32[]{:S(2)}, u32[]{:S(2)}) async-start(bf16[128,16,128]{2,1,0:T(8,128)(2,1)} %bitcast.4), calls=%async_computation | async-start | bytes 1048576 | tf_op jit(solution)/shard_map/all_to_all | solution.py:134
  23.4 0.7 shard_map.94.tiles_ref
  24.1 3.3 %collective-permute-start = (bf16[1552,128]{1,0:T(8,128)(2,1)S(1)}, bf16[1552,128]{1,0:T(8,128)(2,1)S(1)}, u32[]{:S(2)}, u32[]{:S(2)}) collective-permute-start(bf16[1552,128]{1,0:T(8,128)(2,1)S(1)} %shard_map.94.tiles_ref), channel_id=1, source_target_pairs={{0,16},{16,0},{1,17},{17,1},{2,18},{18,2},{3,19},{19,3},{4,20},{20... | collective-permute-start | bytes 1191944 | tf_op jit(solution)/shard_map/ppermute | solution.py:146
  27.4 2.5 %collective-permute-start.2 = (bf16[1552,128]{1,0:T(8,128)(2,1)S(1)}, bf16[1552,128]{1,0:T(8,128)(2,1)S(1)}, u32[]{:S(2)}, u32[]{:S(2)}) collective-permute-start(bf16[1552,128]{1,0:T(8,128)(2,1)S(1)} %shard_map.94.tiles_ref), channel_id=1, source_target_pairs={{0,8},{8,0},{1,9},{9,1},{2,10},{10,2},{3,11},{11,3},{4,12},{12,4},... | collective-permute-start | bytes 1191944 | tf_op jit(solution)/shard_map/ppermute | solution.py:156
  30.0 13.5 %collective-permute-done.tiles_ref = bf16[1552,128]{1,0:T(8,128)(2,1)S(1)} collective-permute-done((bf16[1552,128]{1,0:T(8,128)(2,1)S(1)}, bf16[1552,128]{1,0:T(8,128)(2,1)S(1)}, u32[]{:S(2)}, u32[]{:S(2)}) %collective-permute-start) | collective-permute-done | bytes 397344 | tf_op jit(solution)/shard_map/ppermute | solution.py:146
  43.5 2.8 %collective-permute-start.1 = (bf16[1552,128]{1,0:T(8,128)(2,1)S(1)}, bf16[1552,128]{1,0:T(8,128)(2,1)S(1)}, u32[]{:S(2)}, u32[]{:S(2)}) collective-permute-start(bf16[1552,128]{1,0:T(8,128)(2,1)S(1)} %collective-permute-done.tiles_ref), channel_id=1, source_target_pairs={{0,8},{8,0},{1,9},{9,1},{2,10},{10,2},{3,11},{11,3},{4,12},{12,4},... | collective-permute-start | bytes 1191944 | tf_op jit(solution)/shard_map/ppermute | solution.py:156
  46.3 0.2 shard_map.99
  46.5 0.2 shard_map.97
  46.7 0.2 shard_map.98
  47.0 0.7 collective-permute-done.1.tiles_ref
  47.6 0.2 shard_map.95
  47.8 1.3 convolution_convert_fusion
  49.2 1.3 convolution_convert_fusion.1
  50.5 1.3 convolution_convert_fusion.2
  51.9 1.4 select_bitcast_fusion.3
  53.3 21.0 %all_to_all.25 = bf16[32,16,128]{2,1,0:T(8,128)(2,1)S(1)} all-to-all(bf16[32,16,128]{2,1,0:T(8,128)(2,1)S(1)} %bitcast.78), channel_id=1, replica_groups=mesh['yh'=4,'yl'=2,'xh'=4,'xl'=2,'core'=2,'z'=8] {'xl','core','z'}, dimensions={0} | all-to-all | bytes 262144 | tf_op jit(solution)/shard_map/all_to_all | solution.py:161
  74.3 0.8 shard_map.100
  75.1 15.8 %all_to_all.26 = bf16[32,40,128]{2,1,0:T(8,128)(2,1)S(1)} all-to-all(bf16[32,40,128]{2,1,0:T(8,128)(2,1)S(1)} %get-tuple-element.6), channel_id=1, replica_groups=mesh['yh'=4,'yl'=2,'xh'=4,'xl'=2,'core'=2,'z'=8] {'xl','core','z'}, dimensions={0} | all-to-all | bytes 655360 | tf_op jit(solution)/shard_map/all_to_all | solution.py:176
  91.0 0.2 convolution_bitcast_fusion
  91.3 0.3 fusion.5
  91.6 0.3 convolution_add_fusion.2
  92.0 0.3 convolution_add_fusion.1
  92.3 0.3 fusion
  92.7 0.1 pad_maximum_fusion
  92.8 40.6 %all_to_all.27 = bf16[128,24,128]{2,1,0:T(8,128)(2,1)S(1)} all-to-all(bf16[128,24,128]{2,1,0:T(8,128)(2,1)S(1)} %pad_maximum_fusion), channel_id=1, replica_groups=mesh['yh'=4,'yl'=2,'xh'=4,'xl'=2,'core'=2,'z'=8] {'yh','yl','xh','xl','c..., dimensions={0} | all-to-all | bytes 1572864 | tf_op jit(solution)/shard_map/all_to_all | solution.py:193
  133.6 0.7 broadcast_in_dim.15
  134.2 3.3 %all-to-all-start.4 = ((f32[8,8,512]{2,1,0:T(8,128)}), f32[8,8,512]{2,1,0:T(8,128)S(1)}, u32[]{:S(2)}, u32[]{:S(2)}) async-start(f32[8,8,512]{2,1,0:T(8,128)} %broadcast_in_dim.15), calls=%async_computation.4 | async-start | bytes 262144 | tf_op jit(solution)/shard_map/all_to_all | solution.py:199
  137.6 0.6 pad_maximum_fusion.3
  138.2 4.0 %all-to-all-done.4 = f32[8,8,512]{2,1,0:T(8,128)S(1)} async-done(((f32[8,8,512]{2,1,0:T(8,128)}), f32[8,8,512]{2,1,0:T(8,128)S(1)}, u32[]{:S(2)}, u32[]{:S(2)}) %all-to-all-start.4) | async-done | bytes 131104 | tf_op jit(solution)/shard_map/all_to_all | solution.py:199
  142.2 0.7 copy.23
  (27 shorter events, 0.3 us)
Async XLA Ops:
  0.6 22.8 %copy-start = (s32[1,1,12,128,128]{4,3,2,1,0:T(8,128)S(1)}, s32[1,1,12,128,128]{4,3,2,1,0:T(8,128)}, u32[]{:S(2)}) copy-start(s32[1,1,12,128,128]{4,3,2,1,0:T(8,128)} %param.10) | copy-start | bytes 2359300
  0.6 0.8 copy-start.2
  1.4 21.9 %copy-start.5 = (s32[1,128]{1,0:T(1,128)S(1)}, s32[1,128]{1,0:T(1,128)}, u32[]{:S(2)}) copy-start(s32[1,128]{1,0:T(1,128)} %param.13) | copy-start | bytes 1540
  1.4 22.0 %copy-start.4 = (s32[1,1,12]{2,1,0:T(1,128)S(1)}, s32[1,1,12]{2,1,0:T(1,128)}, u32[]{:S(2)}) copy-start(s32[1,1,12]{2,1,0:T(1,128)} %param.11) | copy-start | bytes 148
  2.4 45.5 %all-to-all-start = ((bf16[128,16,128]{2,1,0:T(8,128)(2,1)}), bf16[128,16,128]{2,1,0:T(8,128)(2,1)}, u32[]{:S(2)}, u32[]{:S(2)}) async-start(bf16[128,16,128]{2,1,0:T(8,128)(2,1)} %bitcast.4), calls=%async_computation | async-start | bytes 1048576 | tf_op jit(solution)/shard_map/all_to_all | solution.py:134
  24.1 19.4 %collective-permute-start = (bf16[1552,128]{1,0:T(8,128)(2,1)S(1)}, bf16[1552,128]{1,0:T(8,128)(2,1)S(1)}, u32[]{:S(2)}, u32[]{:S(2)}) collective-permute-start(bf16[1552,128]{1,0:T(8,128)(2,1)S(1)} %shard_map.94.tiles_ref), channel_id=1, source_target_pairs={{0,16},{16,0},{1,17},{17,1},{2,18},{18,2},{3,19},{19,3},{4,20},{20... | collective-permute-start | bytes 1191944 | tf_op jit(solution)/shard_map/ppermute | solution.py:146
  27.4 19.3 %collective-permute-start.2 = (bf16[1552,128]{1,0:T(8,128)(2,1)S(1)}, bf16[1552,128]{1,0:T(8,128)(2,1)S(1)}, u32[]{:S(2)}, u32[]{:S(2)}) collective-permute-start(bf16[1552,128]{1,0:T(8,128)(2,1)S(1)} %shard_map.94.tiles_ref), channel_id=1, source_target_pairs={{0,8},{8,0},{1,9},{9,1},{2,10},{10,2},{3,11},{11,3},{4,12},{12,4},... | collective-permute-start | bytes 1191944 | tf_op jit(solution)/shard_map/ppermute | solution.py:156
  43.5 4.1 %collective-permute-start.1 = (bf16[1552,128]{1,0:T(8,128)(2,1)S(1)}, bf16[1552,128]{1,0:T(8,128)(2,1)S(1)}, u32[]{:S(2)}, u32[]{:S(2)}) collective-permute-start(bf16[1552,128]{1,0:T(8,128)(2,1)S(1)} %collective-permute-done.tiles_ref), channel_id=1, source_target_pairs={{0,8},{8,0},{1,9},{9,1},{2,10},{10,2},{3,11},{11,3},{4,12},{12,4},... | collective-permute-start | bytes 1191944 | tf_op jit(solution)/shard_map/ppermute | solution.py:156
  51.8 22.4 %copy-start.1 = (bf16[512,512]{1,0:T(8,128)(2,1)S(1)}, bf16[512,512]{1,0:T(8,128)(2,1)}, u32[]{:S(2)}) copy-start(bf16[512,512]{1,0:T(8,128)(2,1)} %weight_ref.1) | copy-start | bytes 1572868
  51.9 22.4 %copy-start.3 = (bf16[1,1,16,512]{3,2,1,0:T(8,128)(2,1)S(1)}, bf16[1,1,16,512]{3,2,1,0:T(8,128)(2,1)}, u32[]{:S(2)}) copy-start(bf16[1,1,16,512]{3,2,1,0:T(8,128)(2,1)} %param.9) | copy-start | bytes 49156
  134.2 7.9 %all-to-all-start.4 = ((f32[8,8,512]{2,1,0:T(8,128)}), f32[8,8,512]{2,1,0:T(8,128)S(1)}, u32[]{:S(2)}, u32[]{:S(2)}) async-start(f32[8,8,512]{2,1,0:T(8,128)} %broadcast_in_dim.15), calls=%async_computation.4 | async-start | bytes 262144 | tf_op jit(solution)/shard_map/all_to_all | solution.py:199

commit v5 on v4

--- a/solution.py
+++ b/solution.py
@@ -74,6 +74,14 @@
         col = jnp.max(place[s : s + 1, :]).astype(jnp.int32)
         start = pl.multiple_of(col * tile_width, tile_width)
         out_ref[:, pl.ds(start, tile_width)] = tiles_ref[s * block_rows : (s + 1) * block_rows, :]
+
+
+def forward_kernel(*refs):
+    *block_refs, panels_ref, out_ref = refs
+    me = lax.axis_index("xl") * 2 + lax.axis_index("core")
+    for other, block_ref in enumerate(block_refs):
+        product = jnp.dot(block_ref[...], panels_ref[...], preferred_element_type=jnp.float32)
+        out_ref[lax.bitwise_xor(me, other)] = product.astype(jnp.bfloat16)
 
 
 def node_kernel(sums_ref, weight_ref, cotangent_ref, active_ref, out_ref):
@@ -156,8 +164,14 @@
         for block in (tiles, lax.ppermute(tiles, "core", SWAP), across, lax.ppermute(across, "core", SWAP))
     ]
 
-    partial = [jnp.dot(b, panels, preferred_element_type=f32).astype(bf16) for b in blocks]
-    partial = jnp.stack(exclusive(partial)).reshape(MEMBERS * depth, node_rows, part)
+    partial = local(
+        forward_kernel,
+        jax.ShapeDtypeStruct((MEMBERS, block_rows, part), bf16),
+        [vmem] * (MEMBERS + 1),
+        2 * MEMBERS * block_rows * col_nodes * part,
+        2 * (MEMBERS * block_rows + part) * col_nodes,
+        [*blocks, panels],
+    ).reshape(MEMBERS * depth, node_rows, part)
     sums = lax.all_to_all(partial, TEAM, 0, 0).reshape(MEMBERS, depth, node_rows, part)
     share = width // depth
     few = node_rows // 2

time: 144 us -> 140 us (0.972)
  blocking collectives: 77.4 us -> 62.1 us
  waiting for transfers between devices: 18.2 us -> 30.5 us
  matrix products: 6.94 us -> 1.58 us
  starting transfers between devices: 32.3 us -> 35.9 us
    all_to_all x1 -> x0, blocking collectives: 15.8 us -> none  [body(): both = lax.all_to_all(both, TEAM, 0, 0)]
    all_to_all x0 -> x1, waiting for transfers between devices: none -> 11.9 us  [body(): both = lax.all_to_all(both, TEAM, 0, 0)]
    dot_general x4 -> x0, matrix products: 5.37 us -> none  [body(): jnp.dot(b, panels, preferred_element_type=f32).astype(bf16)]
    all_to_all x0 -> x1, starting transfers between devices: none -> 4.66 us  [body(): both = lax.all_to_all(both, TEAM, 0, 0)]
    pallas_call x7 -> x8, Pallas kernels: 3.26 us -> 4.24 us  [local(): pl.pallas_call(kernel, out_shape=out, in_specs=[pl.BlockSpec(memory_space...]
  transfers between devices with their start and end apart: 5 -> 6, of which waited for: 3 -> 4; matrix products, arithmetic and copies ran while one was open for 0% -> 0% of each run, Pallas kernels for 1% -> 1%
where the time goes in v5:
time: 140 us; the launch traced here: 139 us
  blocking collectives  62.1 us (44%)
  starting transfers between devices  35.9 us (26%)
  waiting for transfers between devices  30.5 us (22%)
  Pallas kernels  4.24 us (3%)
  local copies, waits for them, and re-layouts  2.21 us (2%)
  matrix products  1.58 us (1%)
  between operations  1.58 us (1%)
    all_to_all x1, blocking collectives, body(): out = lax.all_to_all(jnp.concatenate([grad, term], axis=1), ROW, 0, 0)  40.5 us
    all_to_all x1, blocking collectives, body(): lax.all_to_all(partial, TEAM, 0, 0).reshape(MEMBERS, depth, node_rows, part)  21.6 us
    all_to_all x1, starting transfers between devices, body(): panels = lax.all_to_all(send.reshape(rows, node_rows, part), ROW, 0, 0)  19.3 us
    ppermute x1, waiting for transfers between devices, body(): across = lax.ppermute(tiles, 'xl', SWAP)  14 us
    all_to_all x1, waiting for transfers between devices, body(): both = lax.all_to_all(both, TEAM, 0, 0)  11.9 us
    all_to_all x1, starting transfers between devices, body(): both = lax.all_to_all(both, TEAM, 0, 0)  4.66 us
    pallas_call x8, Pallas kernels, local(): pl.pallas_call(kernel, out_shape=out, in_specs=[pl.BlockSpec(memory_space...  4.24 us
    all_to_all x1, waiting for transfers between devices, body(): lax.all_to_all(jnp.broadcast_to(weight_rows[None], (cube, extra, width)),...  3.99 us
  transfers between devices with their start and end apart: 6, of which 4 were waited for; matrix products, arithmetic and copies ran while one was open for 0% of the time, Pallas kernels for 1%

profile of v5, /device:TPU:1, one launch (start us, length us, event | category | flops | bytes accessed | tf_op | source)
XLA Modules:
  0.0 139.1 jit_solution(887829667854630715)
XLA Ops:
  0.7 0.8 copy-done.2
  1.4 0.9 shard_map.99
  2.3 19.3 %all-to-all-start = ((bf16[128,16,128]{2,1,0:T(8,128)(2,1)}), bf16[128,16,128]{2,1,0:T(8,128)(2,1)S(1)}, u32[]{:S(2)}, u32[]{:S(2)}) async-start(bf16[128,16,128]{2,1,0:T(8,128)(2,1)} %bitcast.4), calls=%async_computation | async-start | bytes 1048576 | tf_op jit(solution)/shard_map/all_to_all | solution.py:142
  22.4 0.7 shard_map.94.tiles_ref
  23.1 3.3 %collective-permute-start.1 = (bf16[1552,128]{1,0:T(8,128)(2,1)S(1)}, bf16[1552,128]{1,0:T(8,128)(2,1)S(1)}, u32[]{:S(2)}, u32[]{:S(2)}) collective-permute-start(bf16[1552,128]{1,0:T(8,128)(2,1)S(1)} %shard_map.94.tiles_ref), channel_id=1, source_target_pairs={{0,16},{16,0},{1,17},{17,1},{2,18},{18,2},{3,19},{19,3},{4,20},{20... | collective-permute-start | bytes 1191944 | tf_op jit(solution)/shard_map/ppermute | solution.py:154
  26.4 2.5 %collective-permute-start = (bf16[1552,128]{1,0:T(8,128)(2,1)S(1)}, bf16[1552,128]{1,0:T(8,128)(2,1)S(1)}, u32[]{:S(2)}, u32[]{:S(2)}) collective-permute-start(bf16[1552,128]{1,0:T(8,128)(2,1)S(1)} %shard_map.94.tiles_ref), channel_id=1, source_target_pairs={{0,8},{8,0},{1,9},{9,1},{2,10},{10,2},{3,11},{11,3},{4,12},{12,4},... | collective-permute-start | bytes 1191944 | tf_op jit(solution)/shard_map/ppermute | solution.py:164
  28.9 14.0 %collective-permute-done.1.tiles_ref = bf16[1552,128]{1,0:T(8,128)(2,1)S(1)} collective-permute-done((bf16[1552,128]{1,0:T(8,128)(2,1)S(1)}, bf16[1552,128]{1,0:T(8,128)(2,1)S(1)}, u32[]{:S(2)}, u32[]{:S(2)}) %collective-permute-start.1) | collective-permute-done | bytes 397344 | tf_op jit(solution)/shard_map/ppermute | solution.py:154
  42.9 2.8 %collective-permute-start.2 = (bf16[1552,128]{1,0:T(8,128)(2,1)S(1)}, bf16[1552,128]{1,0:T(8,128)(2,1)S(1)}, u32[]{:S(2)}, u32[]{:S(2)}) collective-permute-start(bf16[1552,128]{1,0:T(8,128)(2,1)S(1)} %collective-permute-done.1.tiles_ref), channel_id=1, source_target_pairs={{0,8},{8,0},{1,9},{9,1},{2,10},{10,2},{3,11},{11,3},{4,12},{12,4},... | collective-permute-start | bytes 1191944 | tf_op jit(solution)/shard_map/ppermute | solution.py:164
  45.7 0.2 shard_map.95.refs_0_
  45.9 0.2 shard_map.97.refs_2_
  46.1 0.2 shard_map.96.refs_1_
  46.3 0.7 collective-permute-done.2.tiles_ref
  47.0 0.2 shard_map.98.refs_3_
  47.2 0.0 copy-start.1
  47.3 0.7 shard_map.100
  48.0 21.6 %all_to_all.25 = bf16[32,16,128]{2,1,0:T(8,128)(2,1)S(1)} all-to-all(bf16[32,16,128]{2,1,0:T(8,128)(2,1)S(1)} %bitcast.55), channel_id=1, replica_groups=mesh['yh'=4,'yl'=2,'xh'=4,'xl'=2,'core'=2,'z'=8] {'xl','core','z'}, dimensions={0} | all-to-all | bytes 262144 | tf_op jit(solution)/shard_map/all_to_all | solution.py:175
  69.6 1.1 shard_map.101
  70.7 4.7 %all-to-all-start.2 = ((bf16[32,40,128]{2,1,0:T(8,128)(2,1)}), bf16[32,40,128]{2,1,0:T(8,128)(2,1)S(1)}, u32[]{:S(2)}, u32[]{:S(2)}) async-start(bf16[32,40,128]{2,1,0:T(8,128)(2,1)} %get-tuple-element.6), calls=%async_computation.2 | async-start | bytes 655360 | tf_op jit(solution)/shard_map/all_to_all | solution.py:190
  75.4 11.9 %all-to-all-done.2 = bf16[32,40,128]{2,1,0:T(8,128)(2,1)S(1)} async-done(((bf16[32,40,128]{2,1,0:T(8,128)(2,1)}), bf16[32,40,128]{2,1,0:T(8,128)(2,1)S(1)}, u32[]{:S(2)}, u32[]{:S(2)}) %all-to-all-start.2) | async-done | bytes 327712 | tf_op jit(solution)/shard_map/all_to_all | solution.py:190
  87.3 0.2 convolution_bitcast_fusion
  87.6 0.3 fusion.5
  87.9 0.3 convolution_add_fusion.2
  88.3 0.3 convolution_add_fusion.1
  88.6 0.3 fusion
  89.0 0.1 pad_maximum_fusion
  89.1 40.5 %all_to_all.26 = bf16[128,24,128]{2,1,0:T(8,128)(2,1)S(1)} all-to-all(bf16[128,24,128]{2,1,0:T(8,128)(2,1)S(1)} %pad_maximum_fusion), channel_id=1, replica_groups=mesh['yh'=4,'yl'=2,'xh'=4,'xl'=2,'core'=2,'z'=8] {'yh','yl','xh','xl','c..., dimensions={0} | all-to-all | bytes 1572864 | tf_op jit(solution)/shard_map/all_to_all | solution.py:207
  129.7 0.1 slice_reduce_fusion
  129.8 0.7 broadcast_in_dim.15
  130.5 3.3 %all-to-all-start.4 = ((f32[8,8,512]{2,1,0:T(8,128)}), f32[8,8,512]{2,1,0:T(8,128)S(1)}, u32[]{:S(2)}, u32[]{:S(2)}) async-start(f32[8,8,512]{2,1,0:T(8,128)} %broadcast_in_dim.15), calls=%async_computation.4 | async-start | bytes 262144 | tf_op jit(solution)/shard_map/all_to_all | solution.py:213
  133.9 0.6 pad_maximum_fusion.2
  134.5 4.0 %all-to-all-done.4 = f32[8,8,512]{2,1,0:T(8,128)S(1)} async-done(((f32[8,8,512]{2,1,0:T(8,128)}), f32[8,8,512]{2,1,0:T(8,128)S(1)}, u32[]{:S(2)}, u32[]{:S(2)}) %all-to-all-start.4) | async-done | bytes 131104 | tf_op jit(solution)/shard_map/all_to_all | solution.py:213
  138.5 0.7 copy.23
  (24 shorter events, 0.2 us)
Async XLA Ops:
  0.6 21.7 %copy-start = (s32[1,1,12,128,128]{4,3,2,1,0:T(8,128)S(1)}, s32[1,1,12,128,128]{4,3,2,1,0:T(8,128)}, u32[]{:S(2)}) copy-start(s32[1,1,12,128,128]{4,3,2,1,0:T(8,128)} %param.10) | copy-start | bytes 2359300
  0.6 0.8 copy-start.2
  1.4 20.9 %copy-start.5 = (s32[1,128]{1,0:T(1,128)S(1)}, s32[1,128]{1,0:T(1,128)}, u32[]{:S(2)}) copy-start(s32[1,128]{1,0:T(1,128)} %param.13) | copy-start | bytes 1540
  1.4 20.9 %copy-start.4 = (s32[1,1,12]{2,1,0:T(1,128)S(1)}, s32[1,1,12]{2,1,0:T(1,128)}, u32[]{:S(2)}) copy-start(s32[1,1,12]{2,1,0:T(1,128)} %param.11) | copy-start | bytes 148
  2.3 44.9 %all-to-all-start = ((bf16[128,16,128]{2,1,0:T(8,128)(2,1)}), bf16[128,16,128]{2,1,0:T(8,128)(2,1)S(1)}, u32[]{:S(2)}, u32[]{:S(2)}) async-start(bf16[128,16,128]{2,1,0:T(8,128)(2,1)} %bitcast.4), calls=%async_computation | async-start | bytes 1048576 | tf_op jit(solution)/shard_map/all_to_all | solution.py:142
  23.1 19.8 %collective-permute-start.1 = (bf16[1552,128]{1,0:T(8,128)(2,1)S(1)}, bf16[1552,128]{1,0:T(8,128)(2,1)S(1)}, u32[]{:S(2)}, u32[]{:S(2)}) collective-permute-start(bf16[1552,128]{1,0:T(8,128)(2,1)S(1)} %shard_map.94.tiles_ref), channel_id=1, source_target_pairs={{0,16},{16,0},{1,17},{17,1},{2,18},{18,2},{3,19},{19,3},{4,20},{20... | collective-permute-start | bytes 1191944 | tf_op jit(solution)/shard_map/ppermute | solution.py:154
  26.4 19.7 %collective-permute-start = (bf16[1552,128]{1,0:T(8,128)(2,1)S(1)}, bf16[1552,128]{1,0:T(8,128)(2,1)S(1)}, u32[]{:S(2)}, u32[]{:S(2)}) collective-permute-start(bf16[1552,128]{1,0:T(8,128)(2,1)S(1)} %shard_map.94.tiles_ref), channel_id=1, source_target_pairs={{0,8},{8,0},{1,9},{9,1},{2,10},{10,2},{3,11},{11,3},{4,12},{12,4},... | collective-permute-start | bytes 1191944 | tf_op jit(solution)/shard_map/ppermute | solution.py:164
  42.9 4.1 %collective-permute-start.2 = (bf16[1552,128]{1,0:T(8,128)(2,1)S(1)}, bf16[1552,128]{1,0:T(8,128)(2,1)S(1)}, u32[]{:S(2)}, u32[]{:S(2)}) collective-permute-start(bf16[1552,128]{1,0:T(8,128)(2,1)S(1)} %collective-permute-done.1.tiles_ref), channel_id=1, source_target_pairs={{0,8},{8,0},{1,9},{9,1},{2,10},{10,2},{3,11},{11,3},{4,12},{12,4},... | collective-permute-start | bytes 1191944 | tf_op jit(solution)/shard_map/ppermute | solution.py:164
  47.2 22.3 %copy-start.1 = (bf16[512,512]{1,0:T(8,128)(2,1)S(1)}, bf16[512,512]{1,0:T(8,128)(2,1)}, u32[]{:S(2)}) copy-start(bf16[512,512]{1,0:T(8,128)(2,1)} %weight_ref.1) | copy-start | bytes 1572868
  47.3 22.3 %copy-start.3 = (bf16[1,1,16,512]{3,2,1,0:T(8,128)(2,1)S(1)}, bf16[1,1,16,512]{3,2,1,0:T(8,128)(2,1)}, u32[]{:S(2)}) copy-start(bf16[1,1,16,512]{3,2,1,0:T(8,128)(2,1)} %param.9) | copy-start | bytes 49156
  70.7 16.5 %all-to-all-start.2 = ((bf16[32,40,128]{2,1,0:T(8,128)(2,1)}), bf16[32,40,128]{2,1,0:T(8,128)(2,1)S(1)}, u32[]{:S(2)}, u32[]{:S(2)}) async-start(bf16[32,40,128]{2,1,0:T(8,128)(2,1)} %get-tuple-element.6), calls=%async_computation.2 | async-start | bytes 655360 | tf_op jit(solution)/shard_map/all_to_all | solution.py:190
  130.5 7.9 %all-to-all-start.4 = ((f32[8,8,512]{2,1,0:T(8,128)}), f32[8,8,512]{2,1,0:T(8,128)S(1)}, u32[]{:S(2)}, u32[]{:S(2)}) async-start(f32[8,8,512]{2,1,0:T(8,128)} %broadcast_in_dim.15), calls=%async_computation.4 | async-start | bytes 262144 | tf_op jit(solution)/shard_map/all_to_all | solution.py:213

commit v6 on v5

--- a/solution.py
+++ b/solution.py
@@ -12,9 +12,7 @@
 MEMBERS = 4
 
 
-def exclusive(blocks):
-    core = lax.axis_index("core") == 1
-    half = lax.axis_index("xl") == 1
+def exclusive(blocks, core, half):
     a, b, c, d = (blocks[i] for i in range(MEMBERS))
     a, b, c, d = (
         jnp.where(core, b, a),
@@ -151,6 +149,9 @@
         6 * slots * block_rows * tile_width,
         [tile_count[0], tile_cols[0, 0], lax.rsqrt(degree.astype(f32)), tile_mask[0, 0]],
     )
+    tiles, core, half = lax.optimization_barrier(
+        (tiles, lax.axis_index("core") == 1, lax.axis_index("xl") == 1)
+    )
     across = lax.ppermute(tiles, "xl", SWAP)
     blocks = [
         local(
@@ -188,7 +189,7 @@
         [sums, weight, cotangent[0, 0]],
     )
     both = lax.all_to_all(both, TEAM, 0, 0)
-    proj = exclusive(both[:, :node_rows].reshape(MEMBERS, block_rows, part))
+    proj = exclusive(both[:, :node_rows].reshape(MEMBERS, block_rows, part), core, half)
     contract_rows = (((0,), (0,)), ((), ()))
     grad = sum(
         lax.dot_general(b, p, contract_rows, preferred_element_type=f32)
@@ -210,6 +211,7 @@
     feature_grad = jnp.concatenate([total[m] for m in range(MEMBERS)], axis=1).astype(bf16)
     weight_rows = jnp.sum(out[:, :, node_rows:].astype(f32), axis=0)
     weight_rows = jnp.concatenate([weight_rows[m] for m in range(MEMBERS)], axis=1)
+    weight_rows, feature_grad = lax.optimization_barrier((weight_rows, feature_grad))
     weight_grad = lax.all_to_all(jnp.broadcast_to(weight_rows[None], (cube, extra, width)), CUBE, 0, 0)
     return (
         activated.reshape(1, 1, node_rows, width),

time: 140 us -> 138 us (0.986)
  blocking collectives: 62.1 us -> 85.7 us
  waiting for transfers between devices: 30.5 us -> 14.7 us
  starting transfers between devices: 35.9 us -> 27.9 us
    all_to_all x0 -> x2, blocking collectives: none -> 23.5 us  [the longest x1 15.8 us: body(): both = lax.all_to_all(both, TEAM, 0, 0)]
    all_to_all x2 -> x0, waiting for transfers between devices: 15.8 us -> none  [the longest x1 11.9 us: body(): both = lax.all_to_all(both, TEAM, 0, 0)]
    all_to_all x2 -> x0, starting transfers between devices: 7.98 us -> none  [the longest x1 4.66 us: body(): both = lax.all_to_all(both, TEAM, 0, 0)]
  transfers between devices with their start and end apart: 6 -> 4, of which waited for: 4 -> 2; matrix products, arithmetic and copies ran while one was open for 0% -> 0% of each run, Pallas kernels for 1% -> 1%
where the time goes in v6:
time: 138 us
  blocking collectives  85.7 us (62%)
  starting transfers between devices  27.9 us (20%)
  waiting for transfers between devices  14.7 us (11%)
  Pallas kernels  3.95 us (3%)
  matrix products  1.58 us (1%)
  between operations  1.57 us (1%)
  local copies, waits for them, and re-layouts  1.56 us (1%)
    all_to_all x1, blocking collectives, body(): out = lax.all_to_all(jnp.concatenate([grad, term], axis=1), ROW, 0, 0)  40.6 us
    all_to_all x1, blocking collectives, body(): lax.all_to_all(partial, TEAM, 0, 0).reshape(MEMBERS, depth, node_rows, part)  21.6 us
    all_to_all x1, starting transfers between devices, body(): panels = lax.all_to_all(send.reshape(rows, node_rows, part), ROW, 0, 0)  19.3 us
    all_to_all x1, blocking collectives, body(): both = lax.all_to_all(both, TEAM, 0, 0)  15.8 us
    ppermute x1, waiting for transfers between devices, body(): across = lax.ppermute(tiles, 'xl', SWAP)  14 us
    all_to_all x1, blocking collectives, body(): lax.all_to_all(jnp.broadcast_to(weight_rows[None], (cube, extra, width)),...  7.74 us
    pallas_call x8, Pallas kernels, local(): pl.pallas_call(kernel, out_shape=out, in_specs=[pl.BlockSpec(memory_space...  3.95 us
    ppermute x1, starting transfers between devices, body(): across = lax.ppermute(tiles, 'xl', SWAP)  3.3 us
  transfers between devices with their start and end apart: 4, of which 2 were waited for; matrix products, arithmetic and copies ran while one was open for 0% of the time, Pallas kernels for 1%

profile of v6, /device:TPU:1, one launch (start us, length us, event | category | flops | bytes accessed | tf_op | source)
XLA Modules:
  0.0 137.9 jit_solution(3556233684312251481)
XLA Ops:
  0.7 0.8 copy-done.2
  1.4 0.9 shard_map.99
  2.3 19.3 %all-to-all-start = ((bf16[128,16,128]{2,1,0:T(8,128)(2,1)}), bf16[128,16,128]{2,1,0:T(8,128)(2,1)S(1)}, u32[]{:S(2)}, u32[]{:S(2)}) async-start(bf16[128,16,128]{2,1,0:T(8,128)(2,1)} %bitcast.4), calls=%async_computation | async-start | bytes 1048576 | tf_op jit(solution)/shard_map/all_to_all | solution.py:140
  22.4 0.7 shard_map.94.tiles_ref
  23.1 3.3 %collective-permute-start.1 = (bf16[1552,128]{1,0:T(8,128)(2,1)S(1)}, bf16[1552,128]{1,0:T(8,128)(2,1)S(1)}, u32[]{:S(2)}, u32[]{:S(2)}) collective-permute-start(bf16[1552,128]{1,0:T(8,128)(2,1)S(1)} %shard_map.94.tiles_ref), channel_id=1, source_target_pairs={{0,16},{16,0},{1,17},{17,1},{2,18},{18,2},{3,19},{19,3},{4,20},{20... | collective-permute-start | bytes 1191944 | tf_op jit(solution)/shard_map/ppermute | solution.py:155
  26.4 2.5 %collective-permute-start = (bf16[1552,128]{1,0:T(8,128)(2,1)S(1)}, bf16[1552,128]{1,0:T(8,128)(2,1)S(1)}, u32[]{:S(2)}, u32[]{:S(2)}) collective-permute-start(bf16[1552,128]{1,0:T(8,128)(2,1)S(1)} %shard_map.94.tiles_ref), channel_id=1, source_target_pairs={{0,8},{8,0},{1,9},{9,1},{2,10},{10,2},{3,11},{11,3},{4,12},{12,4},... | collective-permute-start | bytes 1191944 | tf_op jit(solution)/shard_map/ppermute | solution.py:165
  28.9 14.0 %collective-permute-done.1.tiles_ref = bf16[1552,128]{1,0:T(8,128)(2,1)S(1)} collective-permute-done((bf16[1552,128]{1,0:T(8,128)(2,1)S(1)}, bf16[1552,128]{1,0:T(8,128)(2,1)S(1)}, u32[]{:S(2)}, u32[]{:S(2)}) %collective-permute-start.1) | collective-permute-done | bytes 397344 | tf_op jit(solution)/shard_map/ppermute | solution.py:155
  42.9 2.8 %collective-permute-start.2 = (bf16[1552,128]{1,0:T(8,128)(2,1)S(1)}, bf16[1552,128]{1,0:T(8,128)(2,1)S(1)}, u32[]{:S(2)}, u32[]{:S(2)}) collective-permute-start(bf16[1552,128]{1,0:T(8,128)(2,1)S(1)} %collective-permute-done.1.tiles_ref), channel_id=1, source_target_pairs={{0,8},{8,0},{1,9},{9,1},{2,10},{10,2},{3,11},{11,3},{4,12},{12,4},... | collective-permute-start | bytes 1191944 | tf_op jit(solution)/shard_map/ppermute | solution.py:165
  45.7 0.2 shard_map.95.refs_0_
  45.9 0.2 shard_map.97.refs_2_
  46.1 0.0 collective-permute-done.tiles_ref
  46.1 0.2 shard_map.96.refs_1_
  46.3 0.7 collective-permute-done.2.tiles_ref
  47.0 0.2 shard_map.98.refs_3_
  47.2 0.0 all-to-all-done
  47.2 0.0 copy-start.1
  47.3 0.0 copy-start.3
  47.3 0.7 shard_map.100
  48.0 21.6 %all_to_all.25 = bf16[32,16,128]{2,1,0:T(8,128)(2,1)S(1)} all-to-all(bf16[32,16,128]{2,1,0:T(8,128)(2,1)S(1)} %bitcast.56), channel_id=1, replica_groups=mesh['yh'=4,'yl'=2,'xh'=4,'xl'=2,'core'=2,'z'=8] {'xl','core','z'}, dimensions={0} | all-to-all | bytes 262144 | tf_op jit(solution)/shard_map/all_to_all | solution.py:176
  69.6 0.8 shard_map.101
  70.4 15.8 %all_to_all.26 = bf16[32,40,128]{2,1,0:T(8,128)(2,1)S(1)} all-to-all(bf16[32,40,128]{2,1,0:T(8,128)(2,1)S(1)} %get-tuple-element.14), channel_id=1, replica_groups=mesh['yh'=4,'yl'=2,'xh'=4,'xl'=2,'core'=2,'z'=8] {'xl','core','z'}, dimensions={0} | all-to-all | bytes 655360 | tf_op jit(solution)/shard_map/all_to_all | solution.py:191
  86.3 0.2 convolution_bitcast_fusion
  86.5 0.3 fusion.5
  86.9 0.3 convolution_add_fusion.2
  87.2 0.3 convolution_add_fusion.1
  87.6 0.3 fusion
  88.0 0.1 pad_maximum_fusion
  88.1 40.6 %all_to_all.27 = bf16[128,24,128]{2,1,0:T(8,128)(2,1)S(1)} all-to-all(bf16[128,24,128]{2,1,0:T(8,128)(2,1)S(1)} %pad_maximum_fusion), channel_id=1, replica_groups=mesh['yh'=4,'yl'=2,'xh'=4,'xl'=2,'core'=2,'z'=8] {'yh','yl','xh','xl','c..., dimensions={0} | all-to-all | bytes 1572864 | tf_op jit(solution)/shard_map/all_to_all | solution.py:208
  128.7 0.1 slice_reduce_fusion
  128.9 0.6 pad_maximum_fusion.3
  129.5 7.7 %all_to_all.28 = f32[8,8,512]{2,1,0:T(8,128)S(1)} all-to-all(f32[8,8,512]{2,1,0:T(8,128)S(1)} %broadcast_in_dim.15), channel_id=1, replica_groups=mesh['yh'=4,'yl'=2,'xh'=4,'xl'=2,'core'=2,'z'=8] {'yl','xl','core'}, dimensions={0} | all-to-all | bytes 262144 | tf_op jit(solution)/shard_map/all_to_all | solution.py:215
  137.2 0.7 copy.23
  (22 shorter events, 0.2 us)
Async XLA Ops:
  0.6 21.7 %copy-start = (s32[1,1,12,128,128]{4,3,2,1,0:T(8,128)S(1)}, s32[1,1,12,128,128]{4,3,2,1,0:T(8,128)}, u32[]{:S(2)}) copy-start(s32[1,1,12,128,128]{4,3,2,1,0:T(8,128)} %param.10) | copy-start | bytes 2359300
  0.6 0.8 copy-start.2
  1.4 20.9 %copy-start.5 = (s32[1,128]{1,0:T(1,128)S(1)}, s32[1,128]{1,0:T(1,128)}, u32[]{:S(2)}) copy-start(s32[1,128]{1,0:T(1,128)} %param.13) | copy-start | bytes 1540
  1.4 20.9 %copy-start.4 = (s32[1,1,12]{2,1,0:T(1,128)S(1)}, s32[1,1,12]{2,1,0:T(1,128)}, u32[]{:S(2)}) copy-start(s32[1,1,12]{2,1,0:T(1,128)} %param.11) | copy-start | bytes 148
  2.3 44.9 %all-to-all-start = ((bf16[128,16,128]{2,1,0:T(8,128)(2,1)}), bf16[128,16,128]{2,1,0:T(8,128)(2,1)S(1)}, u32[]{:S(2)}, u32[]{:S(2)}) async-start(bf16[128,16,128]{2,1,0:T(8,128)(2,1)} %bitcast.4), calls=%async_computation | async-start | bytes 1048576 | tf_op jit(solution)/shard_map/all_to_all | solution.py:140
  23.1 19.8 %collective-permute-start.1 = (bf16[1552,128]{1,0:T(8,128)(2,1)S(1)}, bf16[1552,128]{1,0:T(8,128)(2,1)S(1)}, u32[]{:S(2)}, u32[]{:S(2)}) collective-permute-start(bf16[1552,128]{1,0:T(8,128)(2,1)S(1)} %shard_map.94.tiles_ref), channel_id=1, source_target_pairs={{0,16},{16,0},{1,17},{17,1},{2,18},{18,2},{3,19},{19,3},{4,20},{20... | collective-permute-start | bytes 1191944 | tf_op jit(solution)/shard_map/ppermute | solution.py:155
  26.4 19.7 %collective-permute-start = (bf16[1552,128]{1,0:T(8,128)(2,1)S(1)}, bf16[1552,128]{1,0:T(8,128)(2,1)S(1)}, u32[]{:S(2)}, u32[]{:S(2)}) collective-permute-start(bf16[1552,128]{1,0:T(8,128)(2,1)S(1)} %shard_map.94.tiles_ref), channel_id=1, source_target_pairs={{0,8},{8,0},{1,9},{9,1},{2,10},{10,2},{3,11},{11,3},{4,12},{12,4},... | collective-permute-start | bytes 1191944 | tf_op jit(solution)/shard_map/ppermute | solution.py:165
  42.9 4.1 %collective-permute-start.2 = (bf16[1552,128]{1,0:T(8,128)(2,1)S(1)}, bf16[1552,128]{1,0:T(8,128)(2,1)S(1)}, u32[]{:S(2)}, u32[]{:S(2)}) collective-permute-start(bf16[1552,128]{1,0:T(8,128)(2,1)S(1)} %collective-permute-done.1.tiles_ref), channel_id=1, source_target_pairs={{0,8},{8,0},{1,9},{9,1},{2,10},{10,2},{3,11},{11,3},{4,12},{12,4},... | collective-permute-start | bytes 1191944 | tf_op jit(solution)/shard_map/ppermute | solution.py:165
  47.2 22.3 %copy-start.1 = (bf16[512,512]{1,0:T(8,128)(2,1)S(1)}, bf16[512,512]{1,0:T(8,128)(2,1)}, u32[]{:S(2)}) copy-start(bf16[512,512]{1,0:T(8,128)(2,1)} %weight_ref.1) | copy-start | bytes 1572868
  47.3 22.3 %copy-start.3 = (bf16[1,1,16,512]{3,2,1,0:T(8,128)(2,1)S(1)}, bf16[1,1,16,512]{3,2,1,0:T(8,128)(2,1)}, u32[]{:S(2)}) copy-start(bf16[1,1,16,512]{3,2,1,0:T(8,128)(2,1)} %param.9) | copy-start | bytes 49156
